TPU v7x, 256 devices: a whole 4x4x8 slice. The times are simulated.
256 devices in a mesh: proc: 16 (over y, z_lo), loss: 8 (over x, z_hi), vars: 2 (over core).
Axes of the slice: x: 4, y: 4, z: 8 (z_hi: 2, z_lo: 4; z = z_hi * 4 + z_lo), core: 2. Of those that a mesh axis runs over, the one named last changes fastest.
Arguments:
- tokens: bfloat16 [32, 360, 1536], P('proc'), may hold values from -6 to 6
- shift: int32 [1], replicated, may hold values from 0 to 11
- w_qkv: bfloat16 [1536, 3, 16, 96], P(None, None, ('loss', 'vars')), may hold values from -0.15625 to 0.15625
- w_proj: bfloat16 [16, 96, 1536], replicated, may hold values from -0.15625 to 0.15625
- ln_gain: float32 [1536], replicated, may hold values from 0.1 to 1.9
- w_dec: bfloat16 [64, 4, 4, 1536], P(('loss', 'vars')), may hold values from -0.15625 to 0.15625
- prediction: bfloat16 [64, 128, 1440], P(('loss', 'vars'), 'proc'), may hold values from -6 to 6
- target: float32 [64, 128, 1440], P(('loss', 'vars'), 'proc'), may hold values from -12 to 12
- legendre: float32 [256, 128, 384], P('proc'), may hold values from -0.5 to 0.5
Outputs:
- amse: float32 [64], P(('loss', 'vars'))
- field_grad: float32 [64, 128, 1440], P(('loss', 'vars'), 'proc')
- input_grad: bfloat16 [32, 360, 1536], P('proc', None, ('loss', 'vars'))
Inputs may be any that keep to these rules, and one draw needn't show every extreme that they name: `shift`: the offset is the same for all tokens.
All inputs are finite; a program needn't handle non-finite values.
Results may differ from a plain program's by a relative error of at most 0.012.
Values may be sent and summed in bfloat16 or wider, within the bound.
No kernel may reach another device: no remote copies, remote signals or barrier semaphores. Data moves between devices by JAX's collectives and lax.ppermute only.
A program may use at most 128 MiB of HBM per device.

v0:
```python
import math

import jax
import jax.numpy as jnp
import ml_dtypes
import numpy as np
from jax import lax
from jax.experimental import pallas as pl
from jax.experimental.pallas import tpu as pltpu
from jax.sharding import PartitionSpec as P

HEAD = 96
VARS = 64
LAT = 128
LON = 1440
LDEG = 384
MODES = 256
D = 1536
COLS = 360
WC = 12
GROUP = 48
TOK = 2 * GROUP
PAD = 384
EPSILON = 1e-06
NORM_EPSILON = 1e-05
SCALE = HEAD ** (-0.5)
f32, bf16 = jnp.float32, jnp.bfloat16
MIB = 1 << 20


def split_table(table):
    high = table.astype(ml_dtypes.bfloat16)
    low = (table - high.astype(np.float64)).astype(ml_dtypes.bfloat16)
    return high, low


def fourier_tables():
    column, wavenumber = np.arange(LON), np.arange(MODES)
    phase = (column[:, None] * wavenumber[None, :] % LON) * (2.0 * math.pi / LON)
    basis = np.stack([np.cos(phase), -np.sin(phase)], -1) / math.sqrt(LON)
    forward = split_table(basis.reshape(LON, 2 * MODES))
    back = basis.reshape(LON, 16, 16, 2).transpose(1, 3, 2, 0).reshape(2 * MODES, LON)
    cells = np.zeros((2 * MODES, 4, PAD))
    cells[:, :, :COLS] = back.reshape(2 * MODES, COLS, 4).transpose(0, 2, 1)
    return forward, split_table(back), split_table(cells.reshape(2 * MODES, 4 * PAD))


def dot(a, b):
    return lax.dot_general(a, b, (((1,), (0,)), ((), ())), preferred_element_type=f32)


def dot_nt(a, b):
    return lax.dot_general(a, b, (((1,), (1,)), ((), ())), preferred_element_type=f32)


def halves(x):
    high = x.astype(bf16)
    return high, (x - high.astype(f32)).astype(bf16)


def row_mask(shape):
    return lax.broadcasted_iota(jnp.int32, shape, 0) < 4


def swap_rows(x):
    return pltpu.roll(x, 4, 0)


def fourier_kernel(pred_ref, targ_ref, high_ref, low_ref, out_ref):
    t_high, t_low = halves(targ_ref[...])
    rows = jnp.concatenate([pred_ref[...], t_high, t_low], axis=0)
    a = dot(rows, high_ref[...])
    b = dot(rows[:64], low_ref[...])
    y = jnp.concatenate([a[:32] + b[:32], a[32:64] + a[64:] + b[32:]], axis=0)
    for part in range(32):
        lanes = slice(part * 16, part * 16 + 16)
        out_ref[part * 8 : part * 8 + 8, :] = jnp.concatenate(
            [y[fv * 8 : fv * 8 + 8, lanes] for fv in range(8)], axis=1
        )


def split_kernel(leg_ref, high_ref, low_ref):
    for m in range(16):
        high, low = halves(leg_ref[m])
        high_ref[m] = high
        low_ref[m] = low


def legendre_kernel(spec_ref, high_ref, low_ref, harm_ref, power_ref, turned):
    power = jnp.zeros((8, LDEG), f32)
    cross = jnp.zeros((8, LDEG), f32)
    for half in range(2):
        turned[...] = spec_ref[:, half * 8 : half * 8 + 8, :].reshape(128, 128).T
        for m8 in range(8):
            m = half * 8 + m8
            rows = jnp.concatenate(
                [turned[pl.ds(m8 * 2, 8, stride=16), :], turned[pl.ds(m8 * 2 + 1, 8, stride=16), :]],
                axis=0,
            )
            r_high, r_low = halves(rows)
            both = dot(jnp.concatenate([r_high, r_low], axis=0), high_ref[m])
            h = both[:16] + both[16:] + dot(r_high, low_ref[m])
            harm_ref[m] = h
            h0, h1 = h[:8], h[8:]
            power = power + h0 * h0 + h1 * h1
            cross = cross + h0 * swap_rows(h0) + h1 * swap_rows(h1)
    first = jnp.where(row_mask((8, 128)), cross[:, :128], cross[:, 128:256])
    block = jnp.concatenate([power, first, cross[:, 256:]], axis=1)
    for q in range(16):
        power_ref[q] = block


def grad_kernel(power_ref, harm_ref, high_ref, low_ref, amse_ref, out_ref, grads):
    total = jnp.sum(power_ref[...], axis=0)
    upper = row_mask((8, LDEG))
    own = total[:, :LDEG]
    other = swap_rows(own)
    pp = jnp.where(upper, own, other)
    pt = jnp.where(upper, other, own)
    first = total[:, LDEG : LDEG + 128]
    second = swap_rows(first)
    top = row_mask((8, 128))
    cross = jnp.concatenate(
        [jnp.where(top, first, second), jnp.where(top, second, first), total[:, LDEG + 128 :]], axis=1
    )
    amp_p = jnp.sqrt(pp + EPSILON)
    amp_t = jnp.sqrt(pt + EPSILON)
    largest = jnp.maximum(pp, pt)
    incoherence = 1.0 - cross / (amp_p * amp_t)
    terms = (amp_p - amp_t) ** 2 + 2.0 * largest * incoherence
    amse = jnp.sum(terms, axis=1, keepdims=True) * (1.0 / (LDEG * MODES))
    amse_ref[...] = jnp.broadcast_to(amse, (8, 128))
    share = jnp.where(pp > pt, 1.0, jnp.where(pp == pt, 0.5, 0.0))
    grad_p = (
        (amp_p - amp_t) / amp_p
        + 2.0 * share * incoherence
        + largest * cross / (amp_p * amp_p * amp_p * amp_t)
    )
    grad_c = -2.0 * largest / (amp_p * amp_t)
    weight = LAT * LON / (VARS * LDEG * MODES)
    factor = jnp.where(upper, 2.0 * grad_p, grad_c) * weight
    for m in range(16):
        t0 = factor * harm_ref[m, 0:8, :]
        t1 = factor * harm_ref[m, 8:16, :]
        g = jnp.where(upper, t0 + swap_rows(t0), t1 + swap_rows(t1))
        high = g.astype(bf16).astype(f32)
        rows = jnp.concatenate([high, g - high], axis=0).astype(bf16)
        s = dot_nt(rows, high_ref[m]) + dot_nt(rows, low_ref[m])
        grads[m * 8 : m * 8 + 8, :] = s[:8] + s[8:]
    sorted_rows = jnp.concatenate(
        [grads[pl.ds(c * 4 + v, 16, stride=8), :] for v in range(4) for c in range(2)], axis=0
    )
    out_ref[...] = sorted_rows.T


def field_kernel(shift_ref, band_ref, high_ref, low_ref, cell_ref, field_ref, out_ref, sorted_rows):
    tiles = []
    for v in range(4):
        lanes = slice(v * 32, v * 32 + 32)
        tiles.append(jnp.concatenate([band_ref[q, :, lanes] for q in range(16)], axis=1))
    band = jnp.concatenate(tiles, axis=0)
    b_high, b_low = halves(band)
    a = dot(jnp.concatenate([b_high, b_low], axis=0), high_ref[...])
    field_ref[...] = a[:32] + a[32:] + dot(b_high, low_ref[...])
    for v in range(4):
        sorted_rows[v * 4 : v * 4 + 4, :] = tiles[v][:4]
        sorted_rows[16 + v * 4 : 20 + v * 4, :] = tiles[v][4:]
    s_high, s_low = halves(sorted_rows[...])
    g = dot(jnp.concatenate([s_high, s_low], axis=0), cell_ref[...])
    g = g[:32] + g[32:]
    g = jnp.concatenate(
        [g[r * 16 : r * 16 + 16, o * PAD : o * PAD + PAD] for r in range(2) for o in range(4)], axis=0
    )
    shift = shift_ref[0]
    column = lax.broadcasted_iota(jnp.int32, (128, PAD), 1)
    g = jnp.where(
        column < COLS - shift, pltpu.roll(g, PAD - shift, 1), pltpu.roll(g, COLS - shift, 1)
    )
    g = g.T.astype(bf16)
    for x in range(4):
        for z in range(2):
            for c in range(2):
                at = (x * 2 + c) * GROUP
                out_ref[x * 4 + z * 2 + c] = g[at : at + GROUP]


def forward_kernel(heads_ref, tok_ref, gain_ref, *refs):
    w_refs, proj_ref = refs[:8], refs[8]
    normed_ref, inv_ref, qkv_ref, values_ref, weights_ref, own_ref = refs[9:]
    x = tok_ref[...].astype(f32)
    centred = x - jnp.mean(x, axis=1, keepdims=True)
    inv = lax.rsqrt(jnp.mean(centred * centred, axis=1, keepdims=True) + NORM_EPSILON)
    normed = centred * inv
    normed_ref[...] = normed
    inv_ref[...] = jnp.broadcast_to(inv, (TOK, 128))
    norm_out = (normed * gain_ref[...]).astype(bf16)
    row_window = lax.broadcasted_iota(jnp.int32, (TOK, TOK), 0) // WC
    col_window = lax.broadcasted_iota(jnp.int32, (TOK, TOK), 1) // WC
    same = row_window % 4 == col_window % 4
    for b in range(8):
        qkv = dot_nt(w_refs[b][...], norm_out).astype(bf16)
        qkv_ref[b] = qkv
        keys = qkv[96:192].astype(f32).T.astype(bf16)
        values_ref[b] = qkv[192:].astype(f32).T.astype(bf16)
        scores = dot(keys, qkv[:96]) * SCALE
        weights = jnp.where(same, jnp.exp(scores), 0.0)
        weights_ref[b] = weights / jnp.sum(weights, axis=0, keepdims=True)
        own_ref[b * 96 : b * 96 + 96] = proj_ref[heads_ref[b]]


def backward_kernel(order_ref, flag_ref, cells_ref, gain_ref, *refs):
    w_refs, d_refs = refs[:8], refs[8:16]
    normed_ref, inv_ref, qkv_ref, values_ref, weights_ref, own_ref, out_ref = refs[16:]
    rows = [[], []]
    for p in range(8):
        near = cells_ref[order_ref[2 * p]].astype(f32)
        far = cells_ref[order_ref[2 * p + 1]].astype(f32)
        for r in range(2):
            lanes = slice(r * 64, r * 64 + 64)
            rows[r].append(jnp.concatenate([near[:, lanes], far[:, lanes]], axis=1))
    cells = jnp.concatenate([jnp.concatenate(row, axis=1) for row in rows], axis=0).astype(bf16)
    decoder = jnp.concatenate([ref[...] for ref in d_refs], axis=0)
    token_grad = dot(cells, decoder)
    t_high, t_low = halves(token_grad)
    grad_out = (dot_nt(own_ref[...], t_high) + dot_nt(own_ref[...], t_low)).astype(bf16)
    stacked = []
    for b in range(8):
        g = grad_out[b * 96 : b * 96 + 96]
        q, k = qkv_ref[b, 0:96], qkv_ref[b, 96:192]
        w = weights_ref[b]
        grad_v = dot_nt(g, w.astype(bf16))
        grad_w = dot(values_ref[b], g)
        grad_s = w * (grad_w - jnp.sum(w * grad_w, axis=0, keepdims=True))
        grad_s = (grad_s * SCALE).astype(bf16)
        stacked += [dot(k, grad_s), dot_nt(q, grad_s), grad_v]
    stacked = jnp.concatenate(stacked, axis=0).T.astype(bf16)
    weights = jnp.concatenate([ref[...] for ref in w_refs], axis=0)
    scaled = dot(stacked, weights) * gain_ref[...]
    normed = normed_ref[...]
    mean = jnp.mean(scaled, axis=1, keepdims=True)
    slope = jnp.mean(scaled * normed, axis=1, keepdims=True)
    keep = jnp.where(flag_ref[0] == 0, 1.0, 0.0)
    out = inv_ref[:, :1] * (scaled - mean - normed * slope) + keep * token_grad
    out_ref[...] = out.T.astype(bf16)


def final_kernel(shift_ref, part_ref, out_ref):
    shift = shift_ref[0]
    column = lax.broadcasted_iota(jnp.int32, (96, PAD), 1)
    sums = [
        part_ref[x * 4 + c].astype(f32) + part_ref[x * 4 + 2 + c].astype(f32)
        for x in range(4)
        for c in range(2)
    ]
    for r in range(2):
        y = jnp.concatenate([s[:, r * GROUP : r * GROUP + GROUP] for s in sums], axis=1)
        y = jnp.where(column < shift, pltpu.roll(y, shift + PAD - COLS, 1), pltpu.roll(y, shift, 1))
        out_ref[r] = y[:, :COLS].astype(bf16)


VMEM = pl.BlockSpec(memory_space=pltpu.VMEM)
SMEM = pl.BlockSpec(memory_space=pltpu.SMEM)


def call(kernel, outs, scalars, arrays, scratch=(), mib=16, flops=0, name=None):
    moved = sum(a.size * a.dtype.itemsize for a in arrays)
    moved += sum(math.prod(o.shape) * o.dtype.itemsize for o in jax.tree.leaves(outs))
    return pl.pallas_call(
        kernel,
        out_shape=outs,
        in_specs=[SMEM] * len(scalars) + [VMEM] * len(arrays),
        out_specs=jax.tree.map(lambda _: VMEM, outs),
        scratch_shapes=scratch,
        compiler_params=pltpu.CompilerParams(vmem_limit_bytes=mib * MIB),
        cost_estimate=pl.CostEstimate(flops=flops, bytes_accessed=moved, transcendentals=0),
        name=name,
    )(*scalars, *arrays)


def shape(dims, kind=f32):
    return jax.ShapeDtypeStruct(dims, kind)


def body(tokens, shift, w_qkv, w_proj, ln_gain, w_dec, prediction, target, legendre):
    forward, back, cells = fourier_tables()
    place = lax.axis_index("loss")
    x_at, z_at, core = place // 2, place % 2, lax.axis_index("vars")
    group = ("loss", "vars")
    offset = shift[0]

    def along_x(block, step):
        pairs = [(x * 2 + z, (x + step) % 4 * 2 + z) for x in range(4) for z in range(2)]
        return lax.ppermute(block, "loss", pairs)

    def along_z(block):
        return lax.ppermute(block, "loss", [(i, i ^ 1) for i in range(8)])

    def across(block):
        return lax.ppermute(block, "vars", [(0, 1), (1, 0)])

    w_own = jnp.transpose(w_qkv, (1, 2, 3, 0)).reshape(3 * HEAD, D)
    w_all = [w_own, along_x(w_own, 1), along_x(w_own, 3), along_x(w_own, 2)]
    d_own = jnp.transpose(w_dec, (2, 0, 1, 3)).reshape(64, D)
    d_own = jnp.concatenate([d_own, along_z(d_own)], axis=0)
    d_all = [d_own, along_x(d_own, 1), along_x(d_own, 3), along_x(d_own, 2)]
    w_all = w_all + [across(w) for w in w_all]
    d_all = d_all + [across(d) for d in d_all]
    places = [((x_at + dx) % 4, cc) for cc in (core, 1 - core) for dx in (0, 3, 1, 2)]
    heads = jnp.stack([(x * 2 + z_at) * 2 + c for x, c in places]).astype(jnp.int32)
    order = jnp.stack(
        [(x * 2 + z) * 2 + c for x, c in places for z in (z_at, 1 - z_at)]
    ).astype(jnp.int32)

    spectra = call(
        fourier_kernel,
        shape((256, 128)),
        [],
        [prediction.reshape(32, LON), target.reshape(32, LON), *map(jnp.asarray, forward)],
        flops=2 * 160 * LON * 512,
        name="fourier",
    ).reshape(16, 16, 128)
    at_owners = lax.all_to_all(spectra, "proc", 0, 0, tiled=True)
    leg_high, leg_low = call(
        split_kernel,
        [shape((16, LAT, LDEG), bf16), shape((16, LAT, LDEG), bf16)],
        [],
        [legendre],
        name="split",
    )
    harmonics, powers = call(
        legendre_kernel,
        [shape((16, 16, LDEG)), shape((16, 8, 640))],
        [],
        [at_owners, leg_high, leg_low],
        [pltpu.VMEM((128, 128), f32)],
        flops=2 * 48 * 16 * LAT * LDEG,
        name="legendre",
    )
    powers = lax.all_to_all(powers, "proc", 0, 0, tiled=True)
    amse, grad_spectra = call(
        grad_kernel,
        [shape((8, 128)), shape((128, 128))],
        [],
        [powers, harmonics, leg_high, leg_low],
        [pltpu.VMEM((128, 128), f32)],
        flops=2 * 32 * 16 * LAT * LDEG,
        name="grad",
    )
    banded = lax.all_to_all(grad_spectra.reshape(16, 8, 128), "proc", 0, 0, tiled=True)
    field_grad, cell_grads = call(
        field_kernel,
        [shape((32, LON)), shape((16, GROUP, 128), bf16)],
        [shift],
        [banded, *map(jnp.asarray, back), jnp.asarray(cells[0])],
        [pltpu.VMEM((32, 512), f32)],
        flops=2 * 160 * LON * 512,
        name="field",
    )
    cell_grads = lax.all_to_all(cell_grads, group, 0, 0, tiled=True)

    start = ((x_at * 2 + core) * GROUP + offset) % COLS
    wrapped = jnp.concatenate([tokens, tokens[:, :GROUP]], axis=1)
    own_tokens = lax.dynamic_slice_in_dim(wrapped, start, GROUP, 1).reshape(TOK, D)
    gain = ln_gain.reshape(1, D)
    kept = call(
        forward_kernel,
        [
            shape((TOK, D)),
            shape((TOK, 128)),
            shape((8, 3 * HEAD, TOK), bf16),
            shape((8, TOK, HEAD), bf16),
            shape((8, TOK, TOK)),
            shape((8 * HEAD, D), bf16),
        ],
        [heads],
        [own_tokens, gain, *w_all, w_proj],
        mib=40,
        flops=2 * TOK * D * 8 * 3 * HEAD,
        name="forward",
    )
    parts = call(
        backward_kernel,
        shape((D, TOK), bf16),
        [order, z_at.reshape(1).astype(jnp.int32)],
        [cell_grads, gain, *w_all, *d_all, *kept],
        mib=48,
        flops=2 * TOK * D * (8 * 3 * HEAD + 1024 + 2 * 768),
        name="backward",
    )
    parts = lax.all_to_all(parts.reshape(16, HEAD, TOK), group, 0, 0, tiled=True)
    input_grad = call(
        final_kernel, shape((2, HEAD, COLS), bf16), [shift], [parts], name="final"
    )
    return (
        amse[:4, 0],
        field_grad.reshape(4, 8, LON),
        jnp.transpose(input_grad, (0, 2, 1)),
    )


def solution(mesh):
    return jax.shard_map(
        body,
        mesh=mesh,
        in_specs=(
            P("proc", None, None),
            P(),
            P(None, None, ("loss", "vars"), None),
            P(),
            P(),
            P(("loss", "vars"), None, None, None),
            P(("loss", "vars"), "proc", None),
            P(("loss", "vars"), "proc", None),
            P("proc", None, None),
        ),
        out_specs=(
            P(("loss", "vars")),
            P(("loss", "vars"), "proc", None),
            P("proc", None, ("loss", "vars")),
        ),
        check_vma=False,
    )
```

profile of v0, /device:TPU:72, one launch (start us, length us, event | category | flops | bytes accessed | tf_op | source)
XLA Modules:
  0.0 156.2 jit_solution(9651418877521456050)
XLA Ops:
  0.6 0.0 copy-start.5
  0.6 3.1 %collective-permute-start.2 = (bf16[288,1536]{1,0:T(8,128)(2,1)}, bf16[288,1536]{1,0:T(8,128)(2,1)}, u32[]{:S(2)}, u32[]{:S(2)}) collective-permute-start(bf16[288,1536]{1,0:T(8,128)(2,1)} %bitcast.23.refs_0_), channel_id=1, source_target_pairs={{0,8},{2,10},{4,12},{6,14},{8,0},{10,2},{12,4},{14,6},{1,9},{3,11}... | collective-permute-start | bytes 2654216 | tf_op jit(solution)/shard_map/ppermute | solution.py:293
  3.8 1.1 collective-permute-start.1
  4.9 0.9 collective-permute-start
  5.8 1.0 copy.18
  6.8 0.1 reshape.47
  6.8 5.5 %collective-permute-start.7 = (bf16[64,1536]{1,0:T(8,128)(2,1)S(1)}, bf16[64,1536]{1,0:T(8,128)(2,1)S(1)}, u32[]{:S(2)}, u32[]{:S(2)}) collective-permute-start(bf16[64,1536]{1,0:T(8,128)(2,1)S(1)} %reshape.47), channel_id=1, source_target_pairs={{0,2},{2,0},{4,6},{6,4},{8,10},{10,8},{12,14},{14,12},{1,3},{3,1},... | collective-permute-start | bytes 589832 | tf_op jit(solution)/shard_map/ppermute | solution.py:296
  12.3 0.7 constant_dynamic-update-slice_fusion.1
  13.0 8.0 %collective-permute-done.7 = bf16[64,1536]{1,0:T(8,128)(2,1)S(1)} collective-permute-done((bf16[64,1536]{1,0:T(8,128)(2,1)S(1)}, bf16[64,1536]{1,0:T(8,128)(2,1)S(1)}, u32[]{:S(2)}, u32[]{:S(2)}) %collective-permute-start.7) | collective-permute-done | bytes 196640 | tf_op jit(solution)/shard_map/ppermute | solution.py:296
  21.0 0.7 constant_dynamic-update-slice_fusion.refs_8_
  21.7 0.9 collective-permute-start.10
  22.6 1.4 copy-done.6
  24.0 0.9 copy-done.10
  24.9 0.9 copy-done.11
  25.8 1.6 fourier.1
  27.4 6.7 %all-to-all-start = ((f32[16,16,128]{2,1,0:T(8,128)}), f32[16,16,128]{2,1,0:T(8,128)S(1)}, u32[]{:S(2)}, u32[]{:S(2)}) async-start(f32[16,16,128]{2,1,0:T(8,128)} %bitcast.2), calls=%async_computation | async-start | bytes 262144 | tf_op jit(solution)/shard_map/all_to_all | solution.py:322
  34.1 0.0 collective-permute-start.3
  34.1 0.0 collective-permute-done.2.refs_3_
  34.1 0.5 collective-permute-start.6
  34.6 9.5 %collective-permute-done.1.refs_2_ = bf16[288,1536]{1,0:T(8,128)(2,1)} collective-permute-done((bf16[288,1536]{1,0:T(8,128)(2,1)}, bf16[288,1536]{1,0:T(8,128)(2,1)}, u32[]{:S(2)}, u32[]{:S(2)}) %collective-permute-start.1) | collective-permute-done | bytes 884768 | tf_op jit(solution)/shard_map/ppermute | solution.py:293
  44.2 0.0 collective-permute-start.5
  44.2 7.2 %collective-permute-done.10.refs_11_ = bf16[128,1536]{1,0:T(8,128)(2,1)} collective-permute-done((bf16[128,1536]{1,0:T(8,128)(2,1)}, bf16[128,1536]{1,0:T(8,128)(2,1)}, u32[]{:S(2)}, u32[]{:S(2)}) %collective-permute-start.10) | collective-permute-done | bytes 393248 | tf_op jit(solution)/shard_map/ppermute | solution.py:293
  51.4 2.8 %collective-permute-start.9 = (bf16[128,1536]{1,0:T(8,128)(2,1)}, bf16[128,1536]{1,0:T(8,128)(2,1)}, u32[]{:S(2)}, u32[]{:S(2)}) collective-permute-start(bf16[128,1536]{1,0:T(8,128)(2,1)} %constant_dynamic-update-slice_fusion.refs_8_), channel_id=1, source_target_pairs={{0,12},{2,14},{4,0},{6,2},{8,4},{10,6},{12,8},{14,10},{1,13},{3,15... | collective-permute-start | bytes 1179656 | tf_op jit(solution)/shard_map/ppermute | solution.py:293
  54.1 1.9 %copy-done = f32[16,128,384]{2,1,0:T(8,128)S(1)} copy-done((f32[16,128,384]{2,1,0:T(8,128)S(1)}, f32[16,128,384]{2,1,0:T(8,128)}, u32[]{:S(2)}) %copy-start) | copy-done | bytes 3145752
  56.0 0.5 split.1
  56.5 0.0 all-to-all-done.spec_ref
  56.5 0.8 legendre.1
  57.3 0.7 copy-done.7
  58.1 0.8 copy-done.9
  58.8 8.1 %all-to-all-start.1 = ((f32[16,8,640]{2,1,0:T(8,128)}), f32[16,8,640]{2,1,0:T(8,128)S(1)}, u32[]{:S(2)}, u32[]{:S(2)}) async-start(f32[16,8,640]{2,1,0:T(8,128)} %copy-done.9), calls=%async_computation.1 | async-start | bytes 655360 | tf_op jit(solution)/shard_map/all_to_all | solution.py:339
  66.9 0.1 collective-permute-start.4
  67.0 0.0 collective-permute-done.9.refs_10_
  67.0 0.1 collective-permute-start.8
  67.1 7.7 %all-to-all-done.1.power_ref = f32[16,8,640]{2,1,0:T(8,128)S(1)} async-done(((f32[16,8,640]{2,1,0:T(8,128)}), f32[16,8,640]{2,1,0:T(8,128)S(1)}, u32[]{:S(2)}, u32[]{:S(2)}) %all-to-all-start.1) | async-done | bytes 327712 | tf_op jit(solution)/shard_map/all_to_all | solution.py:339
  74.8 1.0 copy-done.8
  75.8 2.0 %grad.1 = (f32[8,128]{1,0:T(8,128)S(1)}, f32[128,128]{1,0:T(8,128)}) custom-call(f32[16,8,640]{2,1,0:T(8,128)S(1)} %all-to-all-done.1.power_ref, f32[16,16,384]{2,1,0:T(8,128)S(1)} %copy-done.8, bf16[16,128,384]{2,1,0:T(8,128)(2,1)S(1)} %get-tuple-element.17.high_ref, bf16[16,128,384]{2,1,0:T(8,128)(2,1)S(1)} %get-tuple-element.18.low_ref), custom_call_target="tpu_custom_call" | custom-call | flops 50331648 | bytes 3936256 | tf_op jit(solution)/shard_map/grad/pallas_call | solution.py:268
  77.7 0.6 copy-done.14
  78.3 6.7 %all-to-all-start.2 = ((f32[16,8,128]{2,1,0:T(8,128)}), f32[16,8,128]{2,1,0:T(8,128)S(1)}, u32[]{:S(2)}, u32[]{:S(2)}) async-start(f32[16,8,128]{2,1,0:T(8,128)} %bitcast.3), calls=%async_computation.2 | async-start | bytes 131072 | tf_op jit(solution)/shard_map/all_to_all | solution.py:349
  85.0 0.0 collective-permute-done.8.refs_9_
  85.0 0.1 collective-permute-start.11
  85.1 0.5 collective-permute-start.14
  85.6 0.0 collective-permute-done.6.refs_7_
  85.6 0.1 collective-permute-start.13
  85.7 0.4 collective-permute-start.12
  86.8 3.3 %all-to-all-done.2.band_ref = f32[16,8,128]{2,1,0:T(8,128)S(1)} async-done(((f32[16,8,128]{2,1,0:T(8,128)}), f32[16,8,128]{2,1,0:T(8,128)S(1)}, u32[]{:S(2)}, u32[]{:S(2)}) %all-to-all-start.2) | async-done | bytes 65568 | tf_op jit(solution)/shard_map/all_to_all | solution.py:349
  90.1 1.4 copy-done.2
  91.5 1.4 copy-done.3
  92.9 1.4 copy-done.4
  94.3 1.8 %field.1 = (f32[32,1440]{1,0:T(8,128)}, bf16[16,48,128]{2,1,0:T(8,128)(2,1)}) custom-call(s32[1]{0:T(128)} %copy.20.shift_ref, f32[16,8,128]{2,1,0:T(8,128)S(1)} %all-to-all-done.2.band_ref, bf16[512,1440]{1,0:T(8,128)(2,1)S(1)} %copy-done.4, bf16[512,1440]{1,0:T(8,128)(2,1)S(1)} %copy-done.3, bf16[512,1536]{1,0:T(8,128)(2,1)S(1)} %copy-done.2), custom_call_target="tpu_custom_call" | custom-call | flops 235929600 | bytes 4968448 | tf_op jit(solution)/shard_map/field/pallas_call | solution.py:268
  96.2 6.1 %all-to-all-start.3 = ((bf16[16,48,128]{2,1,0:T(8,128)(2,1)}), bf16[16,48,128]{2,1,0:T(8,128)(2,1)S(1)}, u32[]{:S(2)}, u32[]{:S(2)}) async-start(bf16[16,48,128]{2,1,0:T(8,128)(2,1)} %get-tuple-element.24), calls=%async_computation.3 | async-start | bytes 393216 | tf_op jit(solution)/shard_map/all_to_all | solution.py:359
  102.5 0.1 stack.79.heads_ref
  102.6 0.1 stack.78.order_ref
  102.7 1.2 fusion
  103.9 0.0 collective-permute-done.4.refs_5_
  103.9 9.4 %forward.1 = (f32[96,1536]{1,0:T(8,128)S(1)}, f32[96,128]{1,0:T(8,128)S(1)}, bf16[8,288,96]{2,1,0:T(8,128)(2,1)S(1)}, bf16[8,96,96]{2,1,0:T(8,128)(2,1)S(1)}, f3...) custom-call(s32[8]{0:T(128)S(1)} %stack.79.heads_ref, bf16[96,1536]{1,0:T(8,128)(2,1)S(1)} %bitcast.31, ...), custom_call_target="tpu_custom_call" | custom-call | flops 679477248 | bytes 15980544 | tf_op jit(solution)/shard_map/forward/pallas_call | solution.py:268
  113.3 1.4 copy-done.1
  114.7 0.6 copy-done.12
  115.4 0.3 all-to-all-done.3.cells_ref
  115.7 0.8 copy-done.13
  116.5 11.9 %backward.1 = bf16[1536,96]{1,0:T(8,128)(2,1)} custom-call(s32[16]{0:T(128)S(1)} %stack.78.order_ref, s32[1]{0:T(128)} %bitcast.21.flag_ref, bf16[16,48,128]{2,1,0:T(8,128)(2,1)S(1)} %all-to-all-done.3.cells_ref, f32[1,1536]{1,0:T(1,128)S(1)} %reshape.45.gain_ref, bf16[288,1536]{1,0:T(8,128)(2,1)} %bitcast.23.refs_0_, ...), custom_call_target="tpu_custom_call" | custom-call | flops 1434451968 | bytes 14604288 | tf_op jit(solution)/shard_map/backward/pallas_call | solution.py:268
  128.4 9.2 %all-to-all-start.4 = ((bf16[16,96,96]{2,1,0:T(8,128)(2,1)}), bf16[16,96,96]{2,1,0:T(8,128)(2,1)S(1)}, u32[]{:S(2)}, u32[]{:S(2)}) async-start(bf16[16,96,96]{2,1,0:T(8,128)(2,1)} %bitcast.28), calls=%async_computation.4 | async-start | bytes 786432 | tf_op jit(solution)/shard_map/all_to_all | solution.py:390
  137.6 0.6 slice_reduce_fusion
  138.2 16.9 %all-to-all-done.4.part_ref = bf16[16,96,96]{2,1,0:T(8,128)(2,1)S(1)} async-done(((bf16[16,96,96]{2,1,0:T(8,128)(2,1)}), bf16[16,96,96]{2,1,0:T(8,128)(2,1)S(1)}, u32[]{:S(2)}, u32[]{:S(2)}) %all-to-all-start.4) | async-done | bytes 294944 | tf_op jit(solution)/shard_map/all_to_all | solution.py:390
  155.1 1.0 final.1
  (29 shorter events, 0.1 us)
Async XLA Ops:
  0.6 22.0 %copy-start.5 = (bf16[1440,512]{1,0:T(8,128)(2,1)S(1)}, bf16[1440,512]{1,0:T(8,128)(2,1)}, u32[]{:S(2)}) copy-start(bf16[1440,512]{1,0:T(8,128)(2,1)} %constant.87.clone.low_ref) | copy-start | bytes 4423684
  0.6 33.5 %collective-permute-start.2 = (bf16[288,1536]{1,0:T(8,128)(2,1)}, bf16[288,1536]{1,0:T(8,128)(2,1)}, u32[]{:S(2)}, u32[]{:S(2)}) collective-permute-start(bf16[288,1536]{1,0:T(8,128)(2,1)} %bitcast.23.refs_0_), channel_id=1, source_target_pairs={{0,8},{2,10},{4,12},{6,14},{8,0},{10,2},{12,4},{14,6},{1,9},{3,11}... | collective-permute-start | bytes 2654216 | tf_op jit(solution)/shard_map/ppermute | solution.py:293
  3.8 40.4 %collective-permute-start.1 = (bf16[288,1536]{1,0:T(8,128)(2,1)}, bf16[288,1536]{1,0:T(8,128)(2,1)}, u32[]{:S(2)}, u32[]{:S(2)}) collective-permute-start(bf16[288,1536]{1,0:T(8,128)(2,1)} %bitcast.23.refs_0_), channel_id=1, source_target_pairs={{0,12},{2,14},{4,0},{6,2},{8,4},{10,6},{12,8},{14,10},{1,13},{3,15... | collective-permute-start | bytes 2654216 | tf_op jit(solution)/shard_map/ppermute | solution.py:293
  4.9 62.0 %collective-permute-start = (bf16[288,1536]{1,0:T(8,128)(2,1)}, bf16[288,1536]{1,0:T(8,128)(2,1)}, u32[]{:S(2)}, u32[]{:S(2)}) collective-permute-start(bf16[288,1536]{1,0:T(8,128)(2,1)} %bitcast.23.refs_0_), channel_id=1, source_target_pairs={{0,4},{2,6},{4,8},{6,10},{8,12},{10,14},{12,0},{14,2},{1,5},{3,7},... | collective-permute-start | bytes 2654216 | tf_op jit(solution)/shard_map/ppermute | solution.py:293
  6.8 14.2 %collective-permute-start.7 = (bf16[64,1536]{1,0:T(8,128)(2,1)S(1)}, bf16[64,1536]{1,0:T(8,128)(2,1)S(1)}, u32[]{:S(2)}, u32[]{:S(2)}) collective-permute-start(bf16[64,1536]{1,0:T(8,128)(2,1)S(1)} %reshape.47), channel_id=1, source_target_pairs={{0,2},{2,0},{4,6},{6,4},{8,10},{10,8},{12,14},{14,12},{1,3},{3,1},... | collective-permute-start | bytes 589832 | tf_op jit(solution)/shard_map/ppermute | solution.py:296
  21.7 29.7 %collective-permute-start.10 = (bf16[128,1536]{1,0:T(8,128)(2,1)}, bf16[128,1536]{1,0:T(8,128)(2,1)}, u32[]{:S(2)}, u32[]{:S(2)}) collective-permute-start(bf16[128,1536]{1,0:T(8,128)(2,1)} %constant_dynamic-update-slice_fusion.refs_8_), channel_id=1, source_target_pairs={{0,8},{2,10},{4,12},{6,14},{8,0},{10,2},{12,4},{14,6},{1,9},{3,11}... | collective-permute-start | bytes 1179656 | tf_op jit(solution)/shard_map/ppermute | solution.py:293
  22.6 1.4 copy-start.6
  24.0 0.9 copy-start.10
  24.9 0.9 copy-start.11
  27.4 29.1 %all-to-all-start = ((f32[16,16,128]{2,1,0:T(8,128)}), f32[16,16,128]{2,1,0:T(8,128)S(1)}, u32[]{:S(2)}, u32[]{:S(2)}) async-start(f32[16,16,128]{2,1,0:T(8,128)} %bitcast.2), calls=%async_computation | async-start | bytes 262144 | tf_op jit(solution)/shard_map/all_to_all | solution.py:322
  34.1 51.0 %collective-permute-start.3 = (bf16[288,1536]{1,0:T(8,128)(2,1)}, bf16[288,1536]{1,0:T(8,128)(2,1)}, u32[]{:S(2)}, u32[]{:S(2)}) collective-permute-start(bf16[288,1536]{1,0:T(8,128)(2,1)} %bitcast.23.refs_0_), channel_id=1, source_target_pairs={{0,1},{1,0},{2,3},{3,2},{4,5},{5,4},{6,7},{7,6},{8,9},{9,8},{10,11... | collective-permute-start | bytes 2654216 | tf_op jit(solution)/shard_map/ppermute | solution.py:299
  34.1 51.5 %collective-permute-start.6 = (bf16[288,1536]{1,0:T(8,128)(2,1)}, bf16[288,1536]{1,0:T(8,128)(2,1)}, u32[]{:S(2)}, u32[]{:S(2)}) collective-permute-start(bf16[288,1536]{1,0:T(8,128)(2,1)} %collective-permute-done.2.refs_3_), channel_id=1, source_target_pairs={{0,1},{1,0},{2,3},{3,2},{4,5},{5,4},{6,7},{7,6},{8,9},{9,8},{10,11... | collective-permute-start | bytes 2654216 | tf_op jit(solution)/shard_map/ppermute | solution.py:299
  44.2 41.6 %collective-permute-start.5 = (bf16[288,1536]{1,0:T(8,128)(2,1)}, bf16[288,1536]{1,0:T(8,128)(2,1)}, u32[]{:S(2)}, u32[]{:S(2)}) collective-permute-start(bf16[288,1536]{1,0:T(8,128)(2,1)} %collective-permute-done.1.refs_2_), channel_id=1, source_target_pairs={{0,1},{1,0},{2,3},{3,2},{4,5},{5,4},{6,7},{7,6},{8,9},{9,8},{10,11... | collective-permute-start | bytes 2654216 | tf_op jit(solution)/shard_map/ppermute | solution.py:299
  51.4 15.6 %collective-permute-start.9 = (bf16[128,1536]{1,0:T(8,128)(2,1)}, bf16[128,1536]{1,0:T(8,128)(2,1)}, u32[]{:S(2)}, u32[]{:S(2)}) collective-permute-start(bf16[128,1536]{1,0:T(8,128)(2,1)} %constant_dynamic-update-slice_fusion.refs_8_), channel_id=1, source_target_pairs={{0,12},{2,14},{4,0},{6,2},{8,4},{10,6},{12,8},{14,10},{1,13},{3,15... | collective-permute-start | bytes 1179656 | tf_op jit(solution)/shard_map/ppermute | solution.py:293
  54.1 1.9 %copy-start = (f32[16,128,384]{2,1,0:T(8,128)S(1)}, f32[16,128,384]{2,1,0:T(8,128)}, u32[]{:S(2)}) copy-start(f32[16,128,384]{2,1,0:T(8,128)} %leg_ref.1) | copy-start | bytes 9437188
  57.3 0.8 copy-start.7
  58.1 0.8 copy-start.9
  58.8 16.0 %all-to-all-start.1 = ((f32[16,8,640]{2,1,0:T(8,128)}), f32[16,8,640]{2,1,0:T(8,128)S(1)}, u32[]{:S(2)}, u32[]{:S(2)}) async-start(f32[16,8,640]{2,1,0:T(8,128)} %copy-done.9), calls=%async_computation.1 | async-start | bytes 655360 | tf_op jit(solution)/shard_map/all_to_all | solution.py:339
  66.9 37.0 %collective-permute-start.4 = (bf16[288,1536]{1,0:T(8,128)(2,1)}, bf16[288,1536]{1,0:T(8,128)(2,1)}, u32[]{:S(2)}, u32[]{:S(2)}) collective-permute-start(bf16[288,1536]{1,0:T(8,128)(2,1)} %collective-permute-done.refs_1_), channel_id=1, source_target_pairs={{0,1},{1,0},{2,3},{3,2},{4,5},{5,4},{6,7},{7,6},{8,9},{9,8},{10,11... | collective-permute-start | bytes 2654216 | tf_op jit(solution)/shard_map/ppermute | solution.py:299
  67.0 18.0 %collective-permute-start.8 = (bf16[128,1536]{1,0:T(8,128)(2,1)}, bf16[128,1536]{1,0:T(8,128)(2,1)}, u32[]{:S(2)}, u32[]{:S(2)}) collective-permute-start(bf16[128,1536]{1,0:T(8,128)(2,1)} %constant_dynamic-update-slice_fusion.refs_8_), channel_id=1, source_target_pairs={{0,4},{2,6},{4,8},{6,10},{8,12},{10,14},{12,0},{14,2},{1,5},{3,7},... | collective-permute-start | bytes 1179656 | tf_op jit(solution)/shard_map/ppermute | solution.py:293
  74.8 1.0 copy-start.8
  77.7 0.6 copy-start.14
  78.3 11.8 %all-to-all-start.2 = ((f32[16,8,128]{2,1,0:T(8,128)}), f32[16,8,128]{2,1,0:T(8,128)S(1)}, u32[]{:S(2)}, u32[]{:S(2)}) async-start(f32[16,8,128]{2,1,0:T(8,128)} %bitcast.3), calls=%async_computation.2 | async-start | bytes 131072 | tf_op jit(solution)/shard_map/all_to_all | solution.py:349
  85.0 30.3 %collective-permute-start.11 = (bf16[128,1536]{1,0:T(8,128)(2,1)}, bf16[128,1536]{1,0:T(8,128)(2,1)S(1)}, u32[]{:S(2)}, u32[]{:S(2)}) collective-permute-start(bf16[128,1536]{1,0:T(8,128)(2,1)} %constant_dynamic-update-slice_fusion.refs_8_), channel_id=1, source_target_pairs={{0,1},{1,0},{2,3},{3,2},{4,5},{5,4},{6,7},{7,6},{8,9},{9,8},{10,11... | collective-permute-start | bytes 1179656 | tf_op jit(solution)/shard_map/ppermute | solution.py:299
  85.1 30.2 %collective-permute-start.14 = (bf16[128,1536]{1,0:T(8,128)(2,1)}, bf16[128,1536]{1,0:T(8,128)(2,1)S(1)}, u32[]{:S(2)}, u32[]{:S(2)}) collective-permute-start(bf16[128,1536]{1,0:T(8,128)(2,1)} %collective-permute-done.10.refs_11_), channel_id=1, source_target_pairs={{0,1},{1,0},{2,3},{3,2},{4,5},{5,4},{6,7},{7,6},{8,9},{9,8},{10,11... | collective-permute-start | bytes 1179656 | tf_op jit(solution)/shard_map/ppermute | solution.py:299
  85.6 29.7 %collective-permute-start.13 = (bf16[128,1536]{1,0:T(8,128)(2,1)}, bf16[128,1536]{1,0:T(8,128)(2,1)S(1)}, u32[]{:S(2)}, u32[]{:S(2)}) collective-permute-start(bf16[128,1536]{1,0:T(8,128)(2,1)} %collective-permute-done.9.refs_10_), channel_id=1, source_target_pairs={{0,1},{1,0},{2,3},{3,2},{4,5},{5,4},{6,7},{7,6},{8,9},{9,8},{10,11... | collective-permute-start | bytes 1179656 | tf_op jit(solution)/shard_map/ppermute | solution.py:299
  85.7 29.6 %collective-permute-start.12 = (bf16[128,1536]{1,0:T(8,128)(2,1)}, bf16[128,1536]{1,0:T(8,128)(2,1)S(1)}, u32[]{:S(2)}, u32[]{:S(2)}) collective-permute-start(bf16[128,1536]{1,0:T(8,128)(2,1)} %collective-permute-done.8.refs_9_), channel_id=1, source_target_pairs={{0,1},{1,0},{2,3},{3,2},{4,5},{5,4},{6,7},{7,6},{8,9},{9,8},{10,11... | collective-permute-start | bytes 1179656 | tf_op jit(solution)/shard_map/ppermute | solution.py:299
  90.1 1.4 copy-start.2
  91.5 1.4 copy-start.3
  92.9 1.4 copy-start.4
  94.3 8.1 %copy-start.16 = (f32[1536]{0:T(1024)S(1)}, f32[1536]{0:T(1024)}, u32[]{:S(2)}) copy-start(f32[1536]{0:T(1024)} %param.18) | copy-start | bytes 18436
  94.3 8.3 %slice-start = ((bf16[2,360,1536]{2,1,0:T(8,128)(2,1)}), bf16[2,48,1536]{2,1,0:T(8,128)(2,1)S(1)}, s32[]{:S(2)}) async-start(bf16[2,360,1536]{2,1,0:T(8,128)(2,1)} %param.14), calls=%async_computation.5 | async-start | bytes 589824 | tf_op jit(solution)/shard_map/slice | solution.py:362
  96.2 19.5 %all-to-all-start.3 = ((bf16[16,48,128]{2,1,0:T(8,128)(2,1)}), bf16[16,48,128]{2,1,0:T(8,128)(2,1)S(1)}, u32[]{:S(2)}, u32[]{:S(2)}) async-start(bf16[16,48,128]{2,1,0:T(8,128)(2,1)} %get-tuple-element.24), calls=%async_computation.3 | async-start | bytes 393216 | tf_op jit(solution)/shard_map/all_to_all | solution.py:359
  113.3 1.4 copy-start.1
  114.7 0.6 copy-start.12
  115.7 0.8 copy-start.13
  116.5 21.1 %copy-start.15 = (f32[8,128]{1,0:T(8,128)S(1)}, f32[8,128]{1,0:T(8,128)}, u32[]{:S(2)}) copy-start(f32[8,128]{1,0:T(8,128)} %copy-done.14) | copy-start | bytes 12292
  128.4 26.7 %all-to-all-start.4 = ((bf16[16,96,96]{2,1,0:T(8,128)(2,1)}), bf16[16,96,96]{2,1,0:T(8,128)(2,1)S(1)}, u32[]{:S(2)}, u32[]{:S(2)}) async-start(bf16[16,96,96]{2,1,0:T(8,128)(2,1)} %bitcast.28), calls=%async_computation.4 | async-start | bytes 786432 | tf_op jit(solution)/shard_map/all_to_all | solution.py:390
where the time goes:
time: 159 us; the launch traced here: 156 us
  waiting for transfers between devices  53 us (33%)
  starting transfers between devices  52.9 us (33%)
  Pallas kernels  29 us (18%)
  local copies, waits for them, and re-layouts  18.5 us (12%)
  between operations  1.65 us (1%)
    pallas_call x8, Pallas kernels, call(): pl.pallas_call(kernel, out_shape=outs, in_specs=[SMEM] * len(scalars) + [...  29 us
    all_to_all x1, waiting for transfers between devices, body(): lax.all_to_all(parts.reshape(16, HEAD, TOK), group, 0, 0, tiled=True)  16.9 us
    ppermute x6, waiting for transfers between devices, along_x(): return lax.ppermute(block, 'loss', pairs)  16.7 us
    unnamed x35, local copies, waits for them, and re-layouts  15.9 us
    all_to_all x1, starting transfers between devices, body(): lax.all_to_all(parts.reshape(16, HEAD, TOK), group, 0, 0, tiled=True)  9.16 us
    ppermute x6, starting transfers between devices, along_x(): return lax.ppermute(block, 'loss', pairs)  8.9 us
    all_to_all x1, starting transfers between devices, body(): powers = lax.all_to_all(powers, 'proc', 0, 0, tiled=True)  8.09 us
    ppermute x1, waiting for transfers between devices, along_z(): return lax.ppermute(block, 'loss', [(i, i ^ 1) for i in range(8)])  8 us
  transfers between devices with their start and end apart: 20, of which 7 were waited for; matrix products, arithmetic and copies ran while one was open for 3% of the time, Pallas kernels for 10%

commit v1 on v0

v1 whole, which is shorter than its diff:
```python
import math

import jax
import jax.numpy as jnp
import ml_dtypes
import numpy as np
from jax import lax
from jax.experimental import pallas as pl
from jax.experimental.pallas import tpu as pltpu
from jax.sharding import PartitionSpec as P

HEAD = 96
VARS = 64
LAT = 128
LON = 1440
LDEG = 384
MODES = 256
D = 1536
COLS = 360
WC = 12
GROUP = 48
TOK = 2 * GROUP
PAD = 384
EPSILON = 1e-06
NORM_EPSILON = 1e-05
SCALE = HEAD ** (-0.5)
f32, bf16 = jnp.float32, jnp.bfloat16
MIB = 1 << 20
BUSY = 1 << 33


def fourier_tables():
    column, wavenumber = np.arange(LON), np.arange(MODES)
    phase = (column[:, None] * wavenumber[None, :] % LON) * (2.0 * math.pi / LON)
    basis = np.stack([np.cos(phase), -np.sin(phase)], -1) / math.sqrt(LON)
    forward = basis.reshape(LON, 2 * MODES)
    back = basis.reshape(LON, 16, 16, 2).transpose(1, 3, 2, 0).reshape(2 * MODES, LON)
    cells = np.zeros((2 * MODES, 4, PAD))
    cells[:, :, :COLS] = back.reshape(2 * MODES, COLS, 4).transpose(0, 2, 1)
    tables = forward, back, cells.reshape(2 * MODES, 4 * PAD)
    return [jnp.asarray(table.astype(ml_dtypes.bfloat16)) for table in tables]


def dot(a, b):
    return lax.dot_general(a, b, (((1,), (0,)), ((), ())), preferred_element_type=f32)


def dot_nt(a, b):
    return lax.dot_general(a, b, (((1,), (1,)), ((), ())), preferred_element_type=f32)


def halves(x):
    high = x.astype(bf16)
    return high, (x - high.astype(f32)).astype(bf16)


def row_mask(shape):
    return lax.broadcasted_iota(jnp.int32, shape, 0) < 4


def swap_rows(x):
    return pltpu.roll(x, 4, 0)


def fetch(pairs, sems):
    copies = [pltpu.make_async_copy(src, dst, sems.at[i]) for i, (src, dst) in enumerate(pairs)]
    for copy in copies:
        copy.start()
    return copies


def fourier_kernel(pred_ref, targ_ref, table_ref, out_ref, pred, targ, table, sems):
    copies = fetch([(table_ref, table), (targ_ref, targ), (pred_ref, pred)], sems)
    for copy in copies:
        copy.wait()
    t_high, t_low = halves(targ[...])
    y = dot(jnp.concatenate([pred[...], t_high, t_low], axis=0), table[...])
    y = jnp.concatenate([y[:32], y[32:64] + y[64:]], axis=0)
    for part in range(32):
        lanes = slice(part * 16, part * 16 + 16)
        out_ref[part * 8 : part * 8 + 8, :] = jnp.concatenate(
            [y[fv * 8 : fv * 8 + 8, lanes] for fv in range(8)], axis=1
        )


def cast_kernel(leg_ref, out_ref):
    for m in range(16):
        out_ref[m] = leg_ref[m].astype(bf16)


def harmonics(spec_ref, leg_ref, turned, m):
    half, m8 = divmod(m, 8)
    if m8 == 0:
        turned[...] = spec_ref[:, half * 8 : half * 8 + 8, :].reshape(128, 128).T
    rows = [turned[pl.ds(m8 * 2 + c, 8, stride=16), :] for c in range(2)]
    high, low = halves(jnp.concatenate(rows, axis=0))
    both = dot(jnp.concatenate([high, low], axis=0), leg_ref[m])
    both = both[:16] + both[16:]
    return both[:8], both[8:]


def legendre_kernel(spec_ref, leg_ref, power_ref, turned):
    power = jnp.zeros((8, LDEG), f32)
    cross = jnp.zeros((8, LDEG), f32)
    for m in range(16):
        h0, h1 = harmonics(spec_ref, leg_ref, turned, m)
        power = power + h0 * h0 + h1 * h1
        cross = cross + h0 * swap_rows(h0) + h1 * swap_rows(h1)
    first = jnp.where(row_mask((8, 128)), cross[:, :128], cross[:, 128:256])
    block = jnp.concatenate([power, first, cross[:, 256:]], axis=1)
    for q in range(16):
        power_ref[q] = block


def grad_kernel(power_ref, spec_ref, leg_ref, amse_ref, out_ref, turned, grads, loss, sem):
    total = jnp.sum(power_ref[...], axis=0)
    upper = row_mask((8, LDEG))
    own = total[:, :LDEG]
    other = swap_rows(own)
    pp = jnp.where(upper, own, other)
    pt = jnp.where(upper, other, own)
    first = total[:, LDEG : LDEG + 128]
    second = swap_rows(first)
    top = row_mask((8, 128))
    cross = jnp.concatenate(
        [jnp.where(top, first, second), jnp.where(top, second, first), total[:, LDEG + 128 :]], axis=1
    )
    amp_p = jnp.sqrt(pp + EPSILON)
    amp_t = jnp.sqrt(pt + EPSILON)
    largest = jnp.maximum(pp, pt)
    incoherence = 1.0 - cross / (amp_p * amp_t)
    terms = (amp_p - amp_t) ** 2 + 2.0 * largest * incoherence
    amse = jnp.sum(terms, axis=1, keepdims=True) * (1.0 / (LDEG * MODES))
    loss[...] = jnp.broadcast_to(amse, (8, 128))
    copy = pltpu.make_async_copy(loss, amse_ref, sem)
    copy.start()
    share = jnp.where(pp > pt, 1.0, jnp.where(pp == pt, 0.5, 0.0))
    grad_p = (
        (amp_p - amp_t) / amp_p
        + 2.0 * share * incoherence
        + largest * cross / (amp_p * amp_p * amp_p * amp_t)
    )
    grad_c = -2.0 * largest / (amp_p * amp_t)
    weight = LAT * LON / (VARS * LDEG * MODES)
    factor = jnp.where(upper, 2.0 * grad_p, grad_c) * weight
    for m in range(16):
        h0, h1 = harmonics(spec_ref, leg_ref, turned, m)
        t0, t1 = factor * h0, factor * h1
        g = jnp.where(upper, t0 + swap_rows(t0), t1 + swap_rows(t1))
        high = g.astype(bf16).astype(f32)
        s = dot_nt(jnp.concatenate([high, g - high], axis=0).astype(bf16), leg_ref[m])
        grads[m * 8 : m * 8 + 8, :] = s[:8] + s[8:]
    sorted_rows = jnp.concatenate(
        [grads[pl.ds(c * 4 + v, 16, stride=8), :] for v in range(4) for c in range(2)], axis=0
    )
    out_ref[...] = sorted_rows.T
    copy.wait()


def pair_kernel(own_ref, far_ref, out_ref):
    size = own_ref.shape[0]
    out_ref[:size] = own_ref[...]
    out_ref[size:] = far_ref[...]


def table_kernel(tick_ref, table_ref, cell_ref, table, cell, sems):
    for copy in fetch([(cell_ref, cell), (table_ref, table)], sems):
        copy.wait()


def field_kernel(shift_ref, band_ref, table, cell, field_ref, out_ref, field, sorted_rows, sem):
    tiles = []
    for v in range(4):
        lanes = slice(v * 32, v * 32 + 32)
        tiles.append(jnp.concatenate([band_ref[q, :, lanes] for q in range(16)], axis=1))
    for v in range(4):
        sorted_rows[v * 4 : v * 4 + 4, :] = tiles[v][:4]
        sorted_rows[16 + v * 4 : 20 + v * 4, :] = tiles[v][4:]
    b_high, b_low = halves(jnp.concatenate(tiles, axis=0))
    a = dot(jnp.concatenate([b_high, b_low], axis=0), table[...])
    field[...] = a[:32] + a[32:]
    store = pltpu.make_async_copy(field, field_ref, sem)
    store.start()
    s_high, s_low = halves(sorted_rows[...])
    g = dot(jnp.concatenate([s_high, s_low], axis=0), cell[...])
    g = g[:32] + g[32:]
    g = jnp.concatenate(
        [g[r * 16 : r * 16 + 16, o * PAD : o * PAD + PAD] for r in range(2) for o in range(4)], axis=0
    )
    shift = shift_ref[0]
    column = lax.broadcasted_iota(jnp.int32, (128, PAD), 1)
    g = jnp.where(
        column < COLS - shift, pltpu.roll(g, PAD - shift, 1), pltpu.roll(g, COLS - shift, 1)
    )
    g = g.T.astype(bf16)
    for x in range(4):
        for z in range(2):
            for c in range(2):
                at = (x * 2 + c) * GROUP
                out_ref[x * 4 + z * 2 + c] = g[at : at + GROUP]
    store.wait()


def norm_rows(tok_ref, gain_ref):
    x = tok_ref[...].astype(f32)
    centred = x - jnp.mean(x, axis=1, keepdims=True)
    inv = lax.rsqrt(jnp.mean(centred * centred, axis=1, keepdims=True) + NORM_EPSILON)
    return centred * inv, inv


def attention_kernel(gain_ref, cells_ref, tok_ref, proj_ref, *refs):
    w_refs, d_refs, out_ref = refs[:8], refs[8:12], refs[12]
    got, tok, decoder, proj, w, sems = refs[13:]
    place, core = lax.axis_index("loss"), lax.axis_index("vars")
    x_at, z_at = place // 2, place % 2
    places = [((x_at + dx) % 4, c) for c in (core, 1 - core) for dx in (0, 3, 1, 2)]
    first = fetch([(tok_ref, tok), (cells_ref, got)], sems.at[0])
    w_copies = [
        pltpu.make_async_copy(w_refs[b], w.at[pl.ds(b * 288, 288)], sems.at[1, b]) for b in range(8)
    ]
    for copy in w_copies[:4]:
        copy.start()
    gain = gain_ref[...]
    row_window = lax.broadcasted_iota(jnp.int32, (TOK, TOK), 0) // WC
    col_window = lax.broadcasted_iota(jnp.int32, (TOK, TOK), 1) // WC
    same = row_window % 4 == col_window % 4
    first[0].wait()
    x = tok[...].astype(f32)
    centred = x - jnp.mean(x, axis=1, keepdims=True)
    inv = lax.rsqrt(jnp.mean(centred * centred, axis=1, keepdims=True) + NORM_EPSILON)
    normed = centred * inv
    norm_out = (normed * gain).astype(bf16)
    heads = []
    for b in range(8):
        if b % 2 == 0:
            for i in (b, b + 1):
                w_copies[i].wait()
                if i < 4:
                    w_copies[i + 4].start()
            both = dot_nt(w[b * 288 : b * 288 + 576], norm_out).astype(bf16)
        if b == 4:
            d_copies = fetch(
                [(d_refs[i], decoder.at[pl.ds(i * 256, 256)]) for i in range(4)], sems.at[2]
            )
            p_copies = fetch(
                [
                    (proj_ref.at[(x * 2 + z_at) * 2 + c], proj.at[pl.ds(i * 96, 96)])
                    for i, (x, c) in enumerate(places)
                ],
                sems.at[3],
            )
        at = b % 2 * 288
        q, k, v = [both[at + i * 96 : at + i * 96 + 96] for i in range(3)]
        keys = k.astype(f32).T.astype(bf16)
        values = v.astype(f32).T.astype(bf16)
        a = jnp.where(same, jnp.exp(dot(keys, q) * SCALE), 0.0)
        heads.append((q, k, values, a / jnp.sum(a, axis=0, keepdims=True)))
    first[1].wait()
    rows = [[], []]
    for x_from, c_from in [(x_at ^ k, c) for c in (core, 1 - core) for k in range(4)]:
        near = got[(x_from * 2 + z_at) * 2 + c_from].astype(f32)
        far = got[(x_from * 2 + 1 - z_at) * 2 + c_from].astype(f32)
        for r in range(2):
            lanes = slice(r * 64, r * 64 + 64)
            rows[r].append(jnp.concatenate([near[:, lanes], far[:, lanes]], axis=1))
    cells = jnp.concatenate([jnp.concatenate(row, axis=1) for row in rows], axis=0).astype(bf16)
    for copy in d_copies:
        copy.wait()
    token_grad = dot(cells, decoder[...])
    for copy in p_copies:
        copy.wait()
    grad_out = dot_nt(proj[...], token_grad.astype(bf16)).astype(bf16)
    stacked = []
    for b in range(8):
        q, k, values, a = heads[b]
        g = grad_out[b * 96 : b * 96 + 96]
        grad_v = dot_nt(g, a.astype(bf16))
        grad_a = dot(values, g)
        grad_s = a * (grad_a - jnp.sum(a * grad_a, axis=0, keepdims=True))
        grad_s = (grad_s * SCALE).astype(bf16)
        stacked += [dot(k, grad_s), dot_nt(q, grad_s), grad_v]
    stacked = jnp.concatenate(stacked, axis=0).T.astype(bf16)
    scaled = dot(stacked, w[...]) * gain
    mean = jnp.mean(scaled, axis=1, keepdims=True)
    slope = jnp.mean(scaled * normed, axis=1, keepdims=True)
    keep = jnp.where(z_at == 0, 1.0, 0.0)
    out = inv * (scaled - mean - normed * slope) + keep * token_grad
    out = out.T
    packed = []
    for g in range(16):
        tail = out[g * 96 + 72 : g * 96 + 96]
        for part in range(3):
            body = out[g * 96 + part * 24 : g * 96 + part * 24 + 24]
            packed.append(jnp.concatenate([body, tail[:, part * 32 : part * 32 + 32]], axis=1))
    out_ref[...] = jnp.concatenate(packed, axis=0).astype(bf16)


def final_kernel(shift_ref, part_ref, out_ref):
    shift = shift_ref[0]
    column = lax.broadcasted_iota(jnp.int32, (96, PAD), 1)
    parts = part_ref[...].astype(f32)
    sums = []
    for x in range(4):
        for c in range(2):
            at = (x * 4 + c) * 72
            s = parts[at : at + 72] + parts[at + 144 : at + 216]
            tail = jnp.concatenate([s[i * 24 : i * 24 + 24, 96:] for i in range(3)], axis=1)
            sums.append(jnp.concatenate([s[:, :96], tail], axis=0))
    for r in range(2):
        y = jnp.concatenate([s[:, r * GROUP : r * GROUP + GROUP] for s in sums], axis=1)
        y = jnp.where(column < shift, pltpu.roll(y, shift + PAD - COLS, 1), pltpu.roll(y, shift, 1))
        out_ref[r] = y[:, :COLS].astype(bf16)


VMEM = pl.BlockSpec(memory_space=pltpu.VMEM)
SMEM = pl.BlockSpec(memory_space=pltpu.SMEM)
HBM = pl.BlockSpec(memory_space=pltpu.HBM)


def call(kernel, outs, scalars, near, far=(), scratch=(), mib=16, flops=0, name=None, spaces=VMEM):
    arrays = [*near, *far]
    moved = sum(a.size * a.dtype.itemsize for a in arrays)
    moved += sum(math.prod(o.shape) * o.dtype.itemsize for o in jax.tree.leaves(outs))
    if isinstance(outs, list) and not isinstance(spaces, list):
        spaces = [spaces] * len(outs)
    return pl.pallas_call(
        kernel,
        out_shape=outs,
        in_specs=[SMEM] * len(scalars) + [VMEM] * len(near) + [HBM] * len(far),
        out_specs=spaces,
        scratch_shapes=scratch,
        compiler_params=pltpu.CompilerParams(vmem_limit_bytes=mib * MIB),
        cost_estimate=pl.CostEstimate(flops=flops, bytes_accessed=moved, transcendentals=0),
        name=name,
    )(*scalars, *arrays)


def shape(dims, kind=f32):
    return jax.ShapeDtypeStruct(dims, kind)


def body(tokens, shift, w_qkv, w_proj, ln_gain, w_dec, prediction, target, legendre):
    forward, back, cells = fourier_tables()
    place = lax.axis_index("loss")
    x_at, z_at, core = place // 2, place % 2, lax.axis_index("vars")
    group = ("loss", "vars")
    offset = shift[0]

    def along_x(block, step):
        pairs = [(x * 2 + z, (x + step) % 4 * 2 + z) for x in range(4) for z in range(2)]
        return lax.ppermute(block, "loss", pairs)

    def along_z(block):
        return lax.ppermute(block, "loss", [(i, i ^ 1) for i in range(8)])

    def across(block):
        return lax.ppermute(block, "vars", [(0, 1), (1, 0)])

    def after(block, earlier):
        return lax.optimization_barrier((block, earlier))[0]

    w_own = jnp.transpose(w_qkv, (1, 2, 3, 0)).reshape(3 * HEAD, D)
    w_all = [w_own, along_x(w_own, 1), along_x(w_own, 3), along_x(w_own, 2)]
    spectra = call(
        fourier_kernel,
        shape((256, 128)),
        [],
        [],
        [prediction.reshape(32, LON), target.reshape(32, LON), forward],
        scratch=[
            pltpu.VMEM((32, LON), bf16),
            pltpu.VMEM((32, LON), f32),
            pltpu.VMEM((LON, 512), bf16),
            pltpu.SemaphoreType.DMA((3,)),
        ],
        mib=60,
        flops=2 * 160 * LON * 512,
        name="fourier",
    )
    at_owners = lax.all_to_all(spectra.reshape(16, 16, 128), "proc", 0, 0, tiled=True)
    leg = call(
        cast_kernel,
        shape((16, LAT, LDEG), bf16),
        [],
        [after(legendre, spectra)],
        flops=BUSY,
        name="cast",
    )
    d_own = jnp.transpose(w_dec, (2, 0, 1, 3)).reshape(64, D)
    d_far = along_z(after(d_own, leg))
    w_all.append(across(after(w_own, leg)))
    powers = call(
        legendre_kernel,
        shape((16, 8, 640)),
        [],
        [at_owners, leg],
        scratch=[pltpu.VMEM((128, 128), f32)],
        flops=2 * 48 * 16 * LAT * LDEG,
        name="legendre",
    )
    d_own = call(
        pair_kernel,
        shape((128, D), bf16),
        [],
        [*after((d_own, d_far), (powers, w_all[4]))],
        flops=BUSY,
        name="pair",
    )
    d_far = lax.ppermute(d_own, "loss", [(i, i ^ 2) for i in range(8)])
    powers = lax.all_to_all(powers, "proc", 0, 0, tiled=True)
    amse, grad_spectra = call(
        grad_kernel,
        [shape((8, 128)), shape((128, 128))],
        [],
        [after(powers, d_own), at_owners, leg],
        scratch=[
            pltpu.VMEM((128, 128), f32),
            pltpu.VMEM((128, 128), f32),
            pltpu.VMEM((8, 128), f32),
            pltpu.SemaphoreType.DMA,
        ],
        flops=2 * 80 * 16 * LAT * LDEG,
        name="grad",
        spaces=[HBM, VMEM],
    )
    banded = lax.all_to_all(grad_spectra.reshape(16, 8, 128), "proc", 0, 0, tiled=True)
    start = ((x_at * 2 + core) * GROUP + offset) % COLS
    back, cells = call(
        table_kernel,
        [shape((512, LON), bf16), shape((512, 4 * PAD), bf16)],
        [],
        [],
        [after(grad_spectra, w_all[1:3]), back, cells],
        scratch=[pltpu.SemaphoreType.DMA((2,))],
        flops=BUSY,
        name="tables",
    )
    w_all += [across(after(w, back)) for w in w_all[1:3]]
    d_own = call(
        pair_kernel,
        shape((256, D), bf16),
        [],
        [*after((d_own, d_far), grad_spectra)],
        flops=BUSY,
        name="pair2",
    )
    d_far = along_x(d_own, 2)
    d_all = [d_own, d_far, across(after(d_own, back))]
    field_grad, cell_grads = call(
        field_kernel,
        [shape((32, LON)), shape((16, GROUP, 128), bf16)],
        [shift],
        [banded, back, cells],
        scratch=[
            pltpu.VMEM((32, LON), f32),
            pltpu.VMEM((32, 512), f32),
            pltpu.SemaphoreType.DMA,
        ],
        flops=2 * 160 * LON * 512,
        name="field",
        spaces=[HBM, VMEM],
    )
    w_all.append(across(after(w_all[3], cell_grads)))
    own_tokens = after(tokens, cell_grads)
    own_tokens = jnp.concatenate([own_tokens, own_tokens[:, :GROUP]], axis=1)
    own_tokens = lax.dynamic_slice_in_dim(own_tokens, start, GROUP, 1).reshape(TOK, D)
    cell_grads = lax.all_to_all(cell_grads, group, 0, 0, tiled=True)
    d_all.append(across(after(d_far, cell_grads)))
    parts = call(
        attention_kernel,
        shape((16 * 72, 128), bf16),
        [],
        [ln_gain.reshape(1, D)],
        [cell_grads, own_tokens, w_proj, *w_all, *d_all],
        scratch=[
            pltpu.VMEM((16, GROUP, 128), bf16),
            pltpu.VMEM((TOK, D), bf16),
            pltpu.VMEM((1024, D), bf16),
            pltpu.VMEM((8 * HEAD, D), bf16),
            pltpu.VMEM((8 * 3 * HEAD, D), bf16),
            pltpu.SemaphoreType.DMA((4, 8)),
        ],
        mib=60,
        flops=2 * TOK * D * (16 * 3 * HEAD + 1024 + 768),
        name="attention",
    )
    parts = lax.all_to_all(parts.reshape(16, 72, 128), group, 0, 0, tiled=True)
    input_grad = call(
        final_kernel, shape((2, HEAD, COLS), bf16), [shift], [parts.reshape(16 * 72, 128)], name="final"
    )
    return (
        amse[:4, 0],
        field_grad.reshape(4, 8, LON),
        jnp.transpose(input_grad, (0, 2, 1)),
    )


def solution(mesh):
    return jax.shard_map(
        body,
        mesh=mesh,
        in_specs=(
            P("proc", None, None),
            P(),
            P(None, None, ("loss", "vars"), None),
            P(),
            P(),
            P(("loss", "vars"), None, None, None),
            P(("loss", "vars"), "proc", None),
            P(("loss", "vars"), "proc", None),
            P("proc", None, None),
        ),
        out_specs=(
            P(("loss", "vars")),
            P(("loss", "vars"), "proc", None),
            P("proc", None, ("loss", "vars")),
        ),
        check_vma=False,
    )
```

time: 159 us -> 128 us (0.81); the launches traced: 156 us -> 127 us
  local copies, waits for them, and re-layouts: 18.5 us -> 4.73 us
  waiting for transfers between devices: 53 us -> 45.6 us
  Pallas kernels: 29 us -> 24.7 us
  starting transfers between devices: 52.9 us -> 48.7 us
    all_to_all x1, waiting for transfers between devices: 0.33 us -> 16.4 us  [body(): cell_grads = lax.all_to_all(cell_grads, group, 0, 0, tiled=True)]
    unnamed x35 -> x18, local copies, waits for them, and re-layouts: 15.9 us -> 3.37 us
    ppermute x1, waiting for transfers between devices: 8 us -> 0.01 us  [along_z(): return lax.ppermute(block, 'loss', [(i, i ^ 1) for i in range(8)])]
    ppermute x6 -> x4, waiting for transfers between devices: 16.7 us -> 8.99 us  [along_x(): return lax.ppermute(block, 'loss', pairs)]
    all_to_all x1, waiting for transfers between devices: 7.66 us -> 3.07 us  [body(): powers = lax.all_to_all(powers, 'proc', 0, 0, tiled=True)]
    pallas_call x8 -> x10, Pallas kernels: 29 us -> 24.7 us  [call(): pl.pallas_call(kernel, out_shape=outs, in_specs=[SMEM] * len(scalars) + [...]
    all_to_all x2, starting transfers between devices: 15.9 us -> 12.1 us  [the longest x1 8.1 us: body(): lax.all_to_all(spectra.reshape(16, 16, 128), 'proc', 0, 0, tiled=True)]
    all_to_all x2, waiting for transfers between devices: 16.9 us -> 14.8 us  [the longest x1 14.8 us: body(): parts = lax.all_to_all(parts.reshape(16, 72, 128), group, 0, 0, tiled=True)]
  transfers between devices with their start and end apart: 20 -> 17, of which waited for: 7 -> 7; matrix products, arithmetic and copies ran while one was open for 3% -> 3% of each run, Pallas kernels for 10% -> 5%
where the time goes in v1:
time: 128 us; the launch traced here: 127 us
  starting transfers between devices  48.7 us (38%)
  waiting for transfers between devices  45.6 us (36%)
  Pallas kernels  24.7 us (19%)
  local copies, waits for them, and re-layouts  4.73 us (4%)
  other arithmetic  1.9 us (1%)
  between operations  1.5 us (1%)
    pallas_call x10, Pallas kernels, call(): pl.pallas_call(kernel, out_shape=outs, in_specs=[SMEM] * len(scalars) + [...  24.7 us
    all_to_all x1, waiting for transfers between devices, body(): cell_grads = lax.all_to_all(cell_grads, group, 0, 0, tiled=True)  16.4 us
    all_to_all x1, waiting for transfers between devices, body(): parts = lax.all_to_all(parts.reshape(16, 72, 128), group, 0, 0, tiled=True)  14.8 us
    ppermute x4, waiting for transfers between devices, along_x(): return lax.ppermute(block, 'loss', pairs)  8.99 us
    all_to_all x1, starting transfers between devices, body(): lax.all_to_all(spectra.reshape(16, 16, 128), 'proc', 0, 0, tiled=True)  8.1 us
    ppermute x4, starting transfers between devices, along_x(): return lax.ppermute(block, 'loss', pairs)  7.62 us
    all_to_all x1, starting transfers between devices, body(): lax.all_to_all(grad_spectra.reshape(16, 8, 128), 'proc', 0, 0, tiled=True)  7.52 us
    all_to_all x1, starting transfers between devices, body(): powers = lax.all_to_all(powers, 'proc', 0, 0, tiled=True)  7.52 us
  transfers between devices with their start and end apart: 17, of which 7 were waited for; matrix products, arithmetic and copies ran while one was open for 3% of the time, Pallas kernels for 5%

profile of v1, /device:TPU:72, one launch (start us, length us, event | category | flops | bytes accessed | tf_op | source)
XLA Modules:
  0.0 127.2 jit_solution(17322688470742561545)
XLA Ops:
  0.6 2.7 %fourier.1 = f32[256,128]{1,0:T(8,128)} custom-call(bf16[32,1440]{1,0:T(8,128)(2,1)} %bitcast.21, f32[32,1440]{1,0:T(8,128)} %bitcast.18, bf16[1440,512]{1,0:T(8,128)(2,1)} %constant.43.clone.table_ref), custom_call_target="tpu_custom_call" | custom-call | flops 235929600 | bytes 1882112 | tf_op jit(solution)/shard_map/fourier/pallas_call | solution.py:326
  3.4 0.0 copy-start
  3.4 1.9 %copy-done = f32[16,128,384]{2,1,0:T(8,128)S(1)} copy-done((f32[16,128,384]{2,1,0:T(8,128)S(1)}, f32[16,128,384]{2,1,0:T(8,128)}, u32[]{:S(2)}) %copy-start) | copy-done | bytes 3145752
  5.3 0.2 cast.1.leg_ref
  5.4 0.1 collective-permute-start.1
  5.5 8.1 %all-to-all-start = ((f32[16,16,128]{2,1,0:T(8,128)}), f32[16,16,128]{2,1,0:T(8,128)S(1)}, u32[]{:S(2)}, u32[]{:S(2)}) async-start(f32[16,16,128]{2,1,0:T(8,128)} %bitcast.2), calls=%async_computation | async-start | bytes 262144 | tf_op jit(solution)/shard_map/all_to_all | solution.py:380
  13.6 0.0 copy-done.7
  13.6 0.1 copy.16
  13.7 0.1 reshape.42.own_ref
  13.8 4.6 %collective-permute-start = (bf16[64,1536]{1,0:T(8,128)(2,1)S(1)}, bf16[64,1536]{1,0:T(8,128)(2,1)S(1)}, u32[]{:S(2)}, u32[]{:S(2)}) collective-permute-start(bf16[64,1536]{1,0:T(8,128)(2,1)S(1)} %reshape.42.own_ref), channel_id=1, source_target_pairs={{0,2},{2,0},{4,6},{6,4},{8,10},{10,8},{12,14},{14,12},{1,3},{3,1},... | collective-permute-start | bytes 589832 | tf_op jit(solution)/shard_map/ppermute | solution.py:354
  18.4 2.8 %collective-permute-start.3 = (bf16[288,1536]{1,0:T(8,128)(2,1)}, bf16[288,1536]{1,0:T(8,128)(2,1)}, u32[]{:S(2)}, u32[]{:S(2)}) collective-permute-start(bf16[288,1536]{1,0:T(8,128)(2,1)} %bitcast.5.refs_0_), channel_id=1, source_target_pairs={{0,12},{2,14},{4,0},{6,2},{8,4},{10,6},{12,8},{14,10},{1,13},{3,15... | collective-permute-start | bytes 2654216 | tf_op jit(solution)/shard_map/ppermute | solution.py:351
  21.1 0.0 collective-permute-start.2
  21.1 0.0 all-to-all-done.spec_ref
  21.1 1.2 legendre.1
  22.4 7.5 %all-to-all-start.1 = ((f32[16,8,640]{2,1,0:T(8,128)}), f32[16,8,640]{2,1,0:T(8,128)S(1)}, u32[]{:S(2)}, u32[]{:S(2)}) async-start(f32[16,8,640]{2,1,0:T(8,128)} %legendre.1), calls=%async_computation.1 | async-start | bytes 655360 | tf_op jit(solution)/shard_map/all_to_all | solution.py:410
  29.9 0.0 collective-permute-done.far_ref
  29.9 0.0 collective-permute-done.1.refs_4_
  29.9 1.4 %collective-permute-start.8 = (bf16[128,1536]{1,0:T(8,128)(2,1)S(1)}, bf16[128,1536]{1,0:T(8,128)(2,1)S(1)}, u32[]{:S(2)}, u32[]{:S(2)}) collective-permute-start(bf16[128,1536]{1,0:T(8,128)(2,1)S(1)} %pair.1.own_ref), channel_id=1, source_target_pairs={{0,4},{2,6},{4,0},{6,2},{8,12},{10,14},{12,8},{14,10},{1,5},{3,7},... | collective-permute-start | bytes 1179656 | tf_op jit(solution)/shard_map/ppermute | solution.py:409
  31.3 3.4 %collective-permute-start.4 = (bf16[288,1536]{1,0:T(8,128)(2,1)}, bf16[288,1536]{1,0:T(8,128)(2,1)}, u32[]{:S(2)}, u32[]{:S(2)}) collective-permute-start(bf16[288,1536]{1,0:T(8,128)(2,1)} %bitcast.5.refs_0_), channel_id=1, source_target_pairs={{0,8},{2,10},{4,12},{6,14},{8,0},{10,2},{12,4},{14,6},{1,9},{3,11}... | collective-permute-start | bytes 2654216 | tf_op jit(solution)/shard_map/ppermute | solution.py:351
  35.4 3.1 %all-to-all-done.1.power_ref = f32[16,8,640]{2,1,0:T(8,128)S(1)} async-done(((f32[16,8,640]{2,1,0:T(8,128)}), f32[16,8,640]{2,1,0:T(8,128)S(1)}, u32[]{:S(2)}, u32[]{:S(2)}) %all-to-all-start.1) | async-done | bytes 327712 | tf_op jit(solution)/shard_map/all_to_all | solution.py:410
  38.4 2.6 %grad.1 = (f32[8,128]{1,0:T(8,128)S(1)}, f32[128,128]{1,0:T(8,128)}) custom-call(f32[16,8,640]{2,1,0:T(8,128)S(1)} %all-to-all-done.1.power_ref, f32[16,16,128]{2,1,0:T(8,128)S(1)} %all-to-all-done.spec_ref, bf16[16,128,384]{2,1,0:T(8,128)(2,1)S(1)} %cast.1.leg_ref), custom_call_target="tpu_custom_call" | custom-call | flops 125829120 | bytes 2101248 | tf_op jit(solution)/shard_map/grad/pallas_call | solution.py:326
  41.0 0.2 collective-permute-done.3.refs_2_
  41.3 2.3 %collective-permute-done.2.refs_1_ = bf16[288,1536]{1,0:T(8,128)(2,1)} collective-permute-done((bf16[288,1536]{1,0:T(8,128)(2,1)}, bf16[288,1536]{1,0:T(8,128)(2,1)}, u32[]{:S(2)}, u32[]{:S(2)}) %collective-permute-start.2) | collective-permute-done | bytes 884768 | tf_op jit(solution)/shard_map/ppermute | solution.py:351
  43.6 7.5 %all-to-all-start.2 = ((f32[16,8,128]{2,1,0:T(8,128)}), f32[16,8,128]{2,1,0:T(8,128)S(1)}, u32[]{:S(2)}, u32[]{:S(2)}) async-start(f32[16,8,128]{2,1,0:T(8,128)} %bitcast.6), calls=%async_computation.2 | async-start | bytes 131072 | tf_op jit(solution)/shard_map/all_to_all | solution.py:426
  51.1 0.0 copy-start.2
  51.1 0.0 collective-permute-done.8.far_ref
  51.1 0.9 pair2.1.refs_8_
  52.1 1.5 %collective-permute-start.9 = (bf16[256,1536]{1,0:T(8,128)(2,1)}, bf16[256,1536]{1,0:T(8,128)(2,1)}, u32[]{:S(2)}, u32[]{:S(2)}) collective-permute-start(bf16[256,1536]{1,0:T(8,128)(2,1)} %pair2.1.refs_8_), channel_id=1, source_target_pairs={{0,8},{2,10},{4,12},{6,14},{8,0},{10,2},{12,4},{14,6},{1,9},{3,11}... | collective-permute-start | bytes 2359304 | tf_op jit(solution)/shard_map/ppermute | solution.py:351
  53.5 0.0 copy-done.1
  53.5 0.0 copy-done.2
  53.5 0.2 tables.1
  53.8 0.0 copy-start.8
  53.8 0.0 slice-start
  53.8 2.3 %all-to-all-done.2.band_ref = f32[16,8,128]{2,1,0:T(8,128)S(1)} async-done(((f32[16,8,128]{2,1,0:T(8,128)}), f32[16,8,128]{2,1,0:T(8,128)S(1)}, u32[]{:S(2)}, u32[]{:S(2)}) %all-to-all-start.2) | async-done | bytes 65568 | tf_op jit(solution)/shard_map/all_to_all | solution.py:426
  56.1 1.9 %field.1 = (f32[32,1440]{1,0:T(8,128)}, bf16[16,48,128]{2,1,0:T(8,128)(2,1)}) custom-call(s32[1]{0:T(128)} %copy.17.shift_ref, f32[16,8,128]{2,1,0:T(8,128)S(1)} %all-to-all-done.2.band_ref, bf16[512,1440]{1,0:T(8,128)(2,1)S(1)} %get-tuple-element.33.table, bf16[512,1536]{1,0:T(8,128)(2,1)S(1)} %get-tuple-element.34.cell), custom_call_target="tpu_custom_call" | custom-call | flops 235929600 | bytes 3493888 | tf_op jit(solution)/shard_map/field/pallas_call | solution.py:326
  58.0 6.7 %all-to-all-start.3 = ((bf16[16,48,128]{2,1,0:T(8,128)(2,1)}), bf16[16,48,128]{2,1,0:T(8,128)(2,1)S(1)}, u32[]{:S(2)}, u32[]{:S(2)}) async-start(bf16[16,48,128]{2,1,0:T(8,128)(2,1)} %get-tuple-element.36), calls=%async_computation.3 | async-start | bytes 393216 | tf_op jit(solution)/shard_map/all_to_all | solution.py:467
  64.8 0.4 collective-permute-start.5
  65.2 0.2 collective-permute-start.6
  65.4 6.4 %collective-permute-done.4.refs_3_ = bf16[288,1536]{1,0:T(8,128)(2,1)} collective-permute-done((bf16[288,1536]{1,0:T(8,128)(2,1)}, bf16[288,1536]{1,0:T(8,128)(2,1)}, u32[]{:S(2)}, u32[]{:S(2)}) %collective-permute-start.4) | collective-permute-done | bytes 884768 | tf_op jit(solution)/shard_map/ppermute | solution.py:351
  71.8 0.0 collective-permute-start.7
  71.8 0.5 collective-permute-start.10
  72.3 16.4 %all-to-all-done.3.cells_ref = bf16[16,48,128]{2,1,0:T(8,128)(2,1)S(1)} async-done(((bf16[16,48,128]{2,1,0:T(8,128)(2,1)}), bf16[16,48,128]{2,1,0:T(8,128)(2,1)S(1)}, u32[]{:S(2)}, u32[]{:S(2)}) %all-to-all-start.3) | async-done | bytes 196640 | tf_op jit(solution)/shard_map/all_to_all | solution.py:467
  88.7 0.0 collective-permute-done.9.refs_9_
  88.7 0.1 collective-permute-start.11
  88.8 0.0 copy-done.8
  88.8 0.6 reshape.46.gain_ref
  89.4 0.0 slice-done
  89.4 1.9 %fusion = bf16[2,48,1536]{2,1,0:T(8,128)(2,1)} fusion(s32[]{:T(128)S(6)} %select_n.16, bf16[2,360,1536]{2,1,0:T(8,128)(2,1)} %param.12, bf16[2,48,1536]{2,1,0:T(8,128)(2,1)S(1)} %slice-done), kind=kLoop, calls=%fused_computation.2 | loop fusion | flops 589824 | bytes 2801668 | tf_op jit(solution)/shard_map/concatenate | solution.py:465
  91.3 0.0 collective-permute-done.5.refs_5_
  91.3 0.0 collective-permute-done.6.refs_6_
  91.3 0.0 copy-start.4
  91.3 0.0 collective-permute-done.7.refs_7_
  91.3 0.0 copy-start.5
  91.4 0.0 collective-permute-done.10.refs_10_
  91.4 0.0 collective-permute-done.11.refs_11_
  91.4 0.0 copy-done.6
  91.4 0.8 copy-done.3
  92.2 0.3 copy-done.4
  92.6 0.3 copy-done.5
  92.8 13.8 %attention.1 = bf16[1152,128]{1,0:T(8,128)(2,1)} custom-call(f32[1,1536]{1,0:T(1,128)} %reshape.46.gain_ref, bf16[16,48,128]{2,1,0:T(8,128)(2,1)} %copy-done.6, bf16[96,1536]{1,0:T(8,128)(2,1)} %bitcast.16, bf16[16,96,1536]{2,1,0:T(8,128)(2,1)} %proj_ref.1, bf16[288,1536]{1,0:T(8,128)(2,1)} %bitcast.5.refs_0_, ...), custom_call_target="tpu_custom_call" | custom-call | flops 1887436800 | bytes 15734784 | tf_op jit(solution)/shard_map/attention/pallas_call | solution.py:326
  106.7 4.0 %all-to-all-start.4 = ((bf16[16,72,128]{2,1,0:T(8,128)(2,1)}), bf16[16,72,128]{2,1,0:T(8,128)(2,1)S(1)}, u32[]{:S(2)}, u32[]{:S(2)}) async-start(bf16[16,72,128]{2,1,0:T(8,128)(2,1)} %bitcast.17), calls=%async_computation.4 | async-start | bytes 589824 | tf_op jit(solution)/shard_map/all_to_all | solution.py:487
  110.6 0.6 slice_reduce_fusion
  111.3 14.8 %all-to-all-done.4 = bf16[16,72,128]{2,1,0:T(8,128)(2,1)S(1)} async-done(((bf16[16,72,128]{2,1,0:T(8,128)(2,1)}), bf16[16,72,128]{2,1,0:T(8,128)(2,1)S(1)}, u32[]{:S(2)}, u32[]{:S(2)}) %all-to-all-start.4) | async-done | bytes 294944 | tf_op jit(solution)/shard_map/all_to_all | solution.py:487
  126.1 1.1 final.1
  (5 shorter events, 0.0 us)
Async XLA Ops:
  3.4 1.9 %copy-start = (f32[16,128,384]{2,1,0:T(8,128)S(1)}, f32[16,128,384]{2,1,0:T(8,128)}, u32[]{:S(2)}) copy-start(f32[16,128,384]{2,1,0:T(8,128)} %leg_ref) | copy-start | bytes 9437188
  5.3 8.4 %copy-start.7 = (bf16[4,4,4,1536]{3,2,1,0:T(4,128)(2,1)S(1)}, bf16[4,4,4,1536]{3,2,1,0:T(4,128)(2,1)}, u32[]{:S(2)}) copy-start(bf16[4,4,4,1536]{3,2,1,0:T(4,128)(2,1)} %param.17) | copy-start | bytes 589828
  5.4 24.5 %collective-permute-start.1 = (bf16[288,1536]{1,0:T(8,128)(2,1)}, bf16[288,1536]{1,0:T(8,128)(2,1)}, u32[]{:S(2)}, u32[]{:S(2)}) collective-permute-start(bf16[288,1536]{1,0:T(8,128)(2,1)} %bitcast.5.refs_0_), channel_id=1, source_target_pairs={{0,1},{1,0},{2,3},{3,2},{4,5},{5,4},{6,7},{7,6},{8,9},{9,8},{10,11... | collective-permute-start | bytes 2654216 | tf_op jit(solution)/shard_map/ppermute | solution.py:357
  5.5 15.6 %all-to-all-start = ((f32[16,16,128]{2,1,0:T(8,128)}), f32[16,16,128]{2,1,0:T(8,128)S(1)}, u32[]{:S(2)}, u32[]{:S(2)}) async-start(f32[16,16,128]{2,1,0:T(8,128)} %bitcast.2), calls=%async_computation | async-start | bytes 262144 | tf_op jit(solution)/shard_map/all_to_all | solution.py:380
  13.8 16.1 %collective-permute-start = (bf16[64,1536]{1,0:T(8,128)(2,1)S(1)}, bf16[64,1536]{1,0:T(8,128)(2,1)S(1)}, u32[]{:S(2)}, u32[]{:S(2)}) collective-permute-start(bf16[64,1536]{1,0:T(8,128)(2,1)S(1)} %reshape.42.own_ref), channel_id=1, source_target_pairs={{0,2},{2,0},{4,6},{6,4},{8,10},{10,8},{12,14},{14,12},{1,3},{3,1},... | collective-permute-start | bytes 589832 | tf_op jit(solution)/shard_map/ppermute | solution.py:354
  18.4 22.9 %collective-permute-start.3 = (bf16[288,1536]{1,0:T(8,128)(2,1)}, bf16[288,1536]{1,0:T(8,128)(2,1)}, u32[]{:S(2)}, u32[]{:S(2)}) collective-permute-start(bf16[288,1536]{1,0:T(8,128)(2,1)} %bitcast.5.refs_0_), channel_id=1, source_target_pairs={{0,12},{2,14},{4,0},{6,2},{8,4},{10,6},{12,8},{14,10},{1,13},{3,15... | collective-permute-start | bytes 2654216 | tf_op jit(solution)/shard_map/ppermute | solution.py:351
  21.1 22.4 %collective-permute-start.2 = (bf16[288,1536]{1,0:T(8,128)(2,1)}, bf16[288,1536]{1,0:T(8,128)(2,1)}, u32[]{:S(2)}, u32[]{:S(2)}) collective-permute-start(bf16[288,1536]{1,0:T(8,128)(2,1)} %bitcast.5.refs_0_), channel_id=1, source_target_pairs={{0,4},{2,6},{4,8},{6,10},{8,12},{10,14},{12,0},{14,2},{1,5},{3,7},... | collective-permute-start | bytes 2654216 | tf_op jit(solution)/shard_map/ppermute | solution.py:351
  22.4 16.1 %all-to-all-start.1 = ((f32[16,8,640]{2,1,0:T(8,128)}), f32[16,8,640]{2,1,0:T(8,128)S(1)}, u32[]{:S(2)}, u32[]{:S(2)}) async-start(f32[16,8,640]{2,1,0:T(8,128)} %legendre.1), calls=%async_computation.1 | async-start | bytes 655360 | tf_op jit(solution)/shard_map/all_to_all | solution.py:410
  29.9 21.2 %collective-permute-start.8 = (bf16[128,1536]{1,0:T(8,128)(2,1)S(1)}, bf16[128,1536]{1,0:T(8,128)(2,1)S(1)}, u32[]{:S(2)}, u32[]{:S(2)}) collective-permute-start(bf16[128,1536]{1,0:T(8,128)(2,1)S(1)} %pair.1.own_ref), channel_id=1, source_target_pairs={{0,4},{2,6},{4,0},{6,2},{8,12},{10,14},{12,8},{14,10},{1,5},{3,7},... | collective-permute-start | bytes 1179656 | tf_op jit(solution)/shard_map/ppermute | solution.py:409
  31.3 40.5 %collective-permute-start.4 = (bf16[288,1536]{1,0:T(8,128)(2,1)}, bf16[288,1536]{1,0:T(8,128)(2,1)}, u32[]{:S(2)}, u32[]{:S(2)}) collective-permute-start(bf16[288,1536]{1,0:T(8,128)(2,1)} %bitcast.5.refs_0_), channel_id=1, source_target_pairs={{0,8},{2,10},{4,12},{6,14},{8,0},{10,2},{12,4},{14,6},{1,9},{3,11}... | collective-permute-start | bytes 2654216 | tf_op jit(solution)/shard_map/ppermute | solution.py:351
  43.6 12.5 %all-to-all-start.2 = ((f32[16,8,128]{2,1,0:T(8,128)}), f32[16,8,128]{2,1,0:T(8,128)S(1)}, u32[]{:S(2)}, u32[]{:S(2)}) async-start(f32[16,8,128]{2,1,0:T(8,128)} %bitcast.6), calls=%async_computation.2 | async-start | bytes 131072 | tf_op jit(solution)/shard_map/all_to_all | solution.py:426
  51.1 2.4 %copy-start.1 = (bf16[512,1536]{1,0:T(8,128)(2,1)S(1)}, bf16[512,1536]{1,0:T(8,128)(2,1)}, u32[]{:S(2)}) copy-start(bf16[512,1536]{1,0:T(8,128)(2,1)} %constant.45.clone.cell_ref) | copy-start | bytes 4718596
  51.1 2.4 %copy-start.2 = (bf16[512,1440]{1,0:T(8,128)(2,1)S(1)}, bf16[512,1440]{1,0:T(8,128)(2,1)}, u32[]{:S(2)}) copy-start(bf16[512,1440]{1,0:T(8,128)(2,1)} %constant.44.clone.table_ref) | copy-start | bytes 4423684
  52.1 36.6 %collective-permute-start.9 = (bf16[256,1536]{1,0:T(8,128)(2,1)}, bf16[256,1536]{1,0:T(8,128)(2,1)}, u32[]{:S(2)}, u32[]{:S(2)}) collective-permute-start(bf16[256,1536]{1,0:T(8,128)(2,1)} %pair2.1.refs_8_), channel_id=1, source_target_pairs={{0,8},{2,10},{4,12},{6,14},{8,0},{10,2},{12,4},{14,6},{1,9},{3,11}... | collective-permute-start | bytes 2359304 | tf_op jit(solution)/shard_map/ppermute | solution.py:351
  53.8 35.0 %copy-start.8 = (f32[1536]{0:T(1024)S(1)}, f32[1536]{0:T(1024)}, u32[]{:S(2)}) copy-start(f32[1536]{0:T(1024)} %param.16) | copy-start | bytes 18436
  53.8 35.6 %slice-start = ((bf16[2,360,1536]{2,1,0:T(8,128)(2,1)}), bf16[2,48,1536]{2,1,0:T(8,128)(2,1)S(1)}, s32[]{:S(2)}) async-start(bf16[2,360,1536]{2,1,0:T(8,128)(2,1)} %param.12), calls=%async_computation.5 | async-start | bytes 589824 | tf_op jit(solution)/shard_map/slice | solution.py:465
  58.0 30.6 %all-to-all-start.3 = ((bf16[16,48,128]{2,1,0:T(8,128)(2,1)}), bf16[16,48,128]{2,1,0:T(8,128)(2,1)S(1)}, u32[]{:S(2)}, u32[]{:S(2)}) async-start(bf16[16,48,128]{2,1,0:T(8,128)(2,1)} %get-tuple-element.36), calls=%async_computation.3 | async-start | bytes 393216 | tf_op jit(solution)/shard_map/all_to_all | solution.py:467
  64.8 26.6 %collective-permute-start.5 = (bf16[288,1536]{1,0:T(8,128)(2,1)}, bf16[288,1536]{1,0:T(8,128)(2,1)S(1)}, u32[]{:S(2)}, u32[]{:S(2)}) collective-permute-start(bf16[288,1536]{1,0:T(8,128)(2,1)} %collective-permute-done.2.refs_1_), channel_id=1, source_target_pairs={{0,1},{1,0},{2,3},{3,2},{4,5},{5,4},{6,7},{7,6},{8,9},{9,8},{10,11... | collective-permute-start | bytes 2654216 | tf_op jit(solution)/shard_map/ppermute | solution.py:357
  65.2 26.1 %collective-permute-start.6 = (bf16[288,1536]{1,0:T(8,128)(2,1)}, bf16[288,1536]{1,0:T(8,128)(2,1)S(1)}, u32[]{:S(2)}, u32[]{:S(2)}) collective-permute-start(bf16[288,1536]{1,0:T(8,128)(2,1)} %collective-permute-done.3.refs_2_), channel_id=1, source_target_pairs={{0,1},{1,0},{2,3},{3,2},{4,5},{5,4},{6,7},{7,6},{8,9},{9,8},{10,11... | collective-permute-start | bytes 2654216 | tf_op jit(solution)/shard_map/ppermute | solution.py:357
  71.8 19.6 %collective-permute-start.7 = (bf16[288,1536]{1,0:T(8,128)(2,1)}, bf16[288,1536]{1,0:T(8,128)(2,1)S(1)}, u32[]{:S(2)}, u32[]{:S(2)}) collective-permute-start(bf16[288,1536]{1,0:T(8,128)(2,1)} %collective-permute-done.4.refs_3_), channel_id=1, source_target_pairs={{0,1},{1,0},{2,3},{3,2},{4,5},{5,4},{6,7},{7,6},{8,9},{9,8},{10,11... | collective-permute-start | bytes 2654216 | tf_op jit(solution)/shard_map/ppermute | solution.py:357
  71.8 19.6 %collective-permute-start.10 = (bf16[256,1536]{1,0:T(8,128)(2,1)}, bf16[256,1536]{1,0:T(8,128)(2,1)}, u32[]{:S(2)}, u32[]{:S(2)}) collective-permute-start(bf16[256,1536]{1,0:T(8,128)(2,1)} %pair2.1.refs_8_), channel_id=1, source_target_pairs={{0,1},{1,0},{2,3},{3,2},{4,5},{5,4},{6,7},{7,6},{8,9},{9,8},{10,11... | collective-permute-start | bytes 2359304 | tf_op jit(solution)/shard_map/ppermute | solution.py:357
  88.7 2.7 %copy-start.6 = (bf16[16,48,128]{2,1,0:T(8,128)(2,1)}, bf16[16,48,128]{2,1,0:T(8,128)(2,1)S(1)}, u32[]{:S(2)}) copy-start(bf16[16,48,128]{2,1,0:T(8,128)(2,1)S(1)} %all-to-all-done.3.cells_ref) | copy-start | bytes 589828
  88.7 2.7 %collective-permute-start.11 = (bf16[256,1536]{1,0:T(8,128)(2,1)}, bf16[256,1536]{1,0:T(8,128)(2,1)}, u32[]{:S(2)}, u32[]{:S(2)}) collective-permute-start(bf16[256,1536]{1,0:T(8,128)(2,1)} %collective-permute-done.9.refs_9_), channel_id=1, source_target_pairs={{0,1},{1,0},{2,3},{3,2},{4,5},{5,4},{6,7},{7,6},{8,9},{9,8},{10,11... | collective-permute-start | bytes 2359304 | tf_op jit(solution)/shard_map/ppermute | solution.py:357
  91.3 0.9 copy-start.3
  91.3 1.2 copy-start.4
  91.3 1.5 %copy-start.5 = (bf16[288,1536]{1,0:T(8,128)(2,1)}, bf16[288,1536]{1,0:T(8,128)(2,1)S(1)}, u32[]{:S(2)}) copy-start(bf16[288,1536]{1,0:T(8,128)(2,1)S(1)} %collective-permute-done.7.refs_7_) | copy-start | bytes 2654212
  106.7 19.4 %all-to-all-start.4 = ((bf16[16,72,128]{2,1,0:T(8,128)(2,1)}), bf16[16,72,128]{2,1,0:T(8,128)(2,1)S(1)}, u32[]{:S(2)}, u32[]{:S(2)}) async-start(bf16[16,72,128]{2,1,0:T(8,128)(2,1)} %bitcast.17), calls=%async_computation.4 | async-start | bytes 589824 | tf_op jit(solution)/shard_map/all_to_all | solution.py:487

commit v2 on v1

--- a/solution.py
+++ b/solution.py
@@ -388,7 +388,6 @@
     )
     d_own = jnp.transpose(w_dec, (2, 0, 1, 3)).reshape(64, D)
     d_far = along_z(after(d_own, leg))
-    w_all.append(across(after(w_own, leg)))
     powers = call(
         legendre_kernel,
         shape((16, 8, 640)),
@@ -402,17 +401,18 @@
         pair_kernel,
         shape((128, D), bf16),
         [],
-        [*after((d_own, d_far), (powers, w_all[4]))],
+        [*after((d_own, d_far), (powers, w_all[1:3]))],
         flops=BUSY,
         name="pair",
     )
     d_far = lax.ppermute(d_own, "loss", [(i, i ^ 2) for i in range(8)])
+    w_all += [across(after(w, d_own)) for w in w_all[:3]]
     powers = lax.all_to_all(powers, "proc", 0, 0, tiled=True)
     amse, grad_spectra = call(
         grad_kernel,
         [shape((8, 128)), shape((128, 128))],
         [],
-        [after(powers, d_own), at_owners, leg],
+        [after(powers, (d_own, w_all[1:3])), at_owners, leg],
         scratch=[
             pltpu.VMEM((128, 128), f32),
             pltpu.VMEM((128, 128), f32),
@@ -435,7 +435,6 @@
         flops=BUSY,
         name="tables",
     )
-    w_all += [across(after(w, back)) for w in w_all[1:3]]
     d_own = call(
         pair_kernel,
         shape((256, D), bf16),
@@ -445,7 +444,7 @@
         name="pair2",
     )
     d_far = along_x(d_own, 2)
-    d_all = [d_own, d_far, across(after(d_own, back))]
+    d_all = [d_own, d_far, across(after(d_own, (back, w_all[4])))]
     field_grad, cell_grads = call(
         field_kernel,
         [shape((32, LON)), shape((16, GROUP, 128), bf16)],
@@ -465,12 +464,13 @@
     own_tokens = jnp.concatenate([own_tokens, own_tokens[:, :GROUP]], axis=1)
     own_tokens = lax.dynamic_slice_in_dim(own_tokens, start, GROUP, 1).reshape(TOK, D)
     cell_grads = lax.all_to_all(cell_grads, group, 0, 0, tiled=True)
-    d_all.append(across(after(d_far, cell_grads)))
+    gain = ln_gain.reshape(1, D)
+    d_all.append(across(after(d_far, (cell_grads, own_tokens, gain))))
     parts = call(
         attention_kernel,
         shape((16 * 72, 128), bf16),
         [],
-        [ln_gain.reshape(1, D)],
+        [gain],
         [cell_grads, own_tokens, w_proj, *w_all, *d_all],
         scratch=[
             pltpu.VMEM((16, GROUP, 128), bf16),

time: 128 us -> 119 us (0.930)
  waiting for transfers between devices: 45.6 us -> 35.7 us
  starting transfers between devices: 48.7 us -> 50.3 us
    ppermute x4, waiting for transfers between devices: 8.99 us -> 0.01 us  [along_x(): return lax.ppermute(block, 'loss', pairs)]
    all_to_all x1, waiting for transfers between devices: 14.8 us -> 11.7 us  [body(): parts = lax.all_to_all(parts.reshape(16, 72, 128), group, 0, 0, tiled=True)]
    all_to_all x1, starting transfers between devices: 3.97 us -> 7.04 us  [body(): parts = lax.all_to_all(parts.reshape(16, 72, 128), group, 0, 0, tiled=True)]
    ppermute x6, waiting for transfers between devices: 0.02 us -> 2.47 us  [across(): return lax.ppermute(block, 'vars', [(0, 1), (1, 0)])]
    all_to_all x1, waiting for transfers between devices: 16.4 us -> 15 us  [body(): cell_grads = lax.all_to_all(cell_grads, group, 0, 0, tiled=True)]
  transfers between devices with their start and end apart: 17 -> 17, of which waited for: 7 -> 6; matrix products, arithmetic and copies ran while one was open for 3% -> 3% of each run, Pallas kernels for 5% -> 8%
where the time goes in v2:
time: 119 us; the launch traced here: 118 us
  starting transfers between devices  50.3 us (42%)
  waiting for transfers between devices  35.7 us (30%)
  Pallas kernels  24.8 us (21%)
  local copies, waits for them, and re-layouts  4.03 us (3%)
  other arithmetic  1.9 us (2%)
  between operations  1.51 us (1%)
    pallas_call x10, Pallas kernels, call(): pl.pallas_call(kernel, out_shape=outs, in_specs=[SMEM] * len(scalars) + [...  24.8 us
    all_to_all x1, waiting for transfers between devices, body(): cell_grads = lax.all_to_all(cell_grads, group, 0, 0, tiled=True)  15 us
    all_to_all x1, waiting for transfers between devices, body(): parts = lax.all_to_all(parts.reshape(16, 72, 128), group, 0, 0, tiled=True)  11.7 us
    all_to_all x1, starting transfers between devices, body(): lax.all_to_all(spectra.reshape(16, 16, 128), 'proc', 0, 0, tiled=True)  8.1 us
    ppermute x4, starting transfers between devices, along_x(): return lax.ppermute(block, 'loss', pairs)  7.85 us
    all_to_all x1, starting transfers between devices, body(): powers = lax.all_to_all(powers, 'proc', 0, 0, tiled=True)  7.52 us
    all_to_all x1, starting transfers between devices, body(): cell_grads = lax.all_to_all(cell_grads, group, 0, 0, tiled=True)  7.13 us
    all_to_all x1, starting transfers between devices, body(): parts = lax.all_to_all(parts.reshape(16, 72, 128), group, 0, 0, tiled=True)  7.04 us
  transfers between devices with their start and end apart: 17, of which 6 were waited for; matrix products, arithmetic and copies ran while one was open for 3% of the time, Pallas kernels for 8%

profile of v2, /device:TPU:72, one launch (start us, length us, event | category | flops | bytes accessed | tf_op | source)
XLA Modules:
  0.0 118.2 jit_solution(3509392668710174842)
XLA Ops:
  0.6 1.6 %collective-permute-start.1 = (bf16[288,1536]{1,0:T(8,128)(2,1)}, bf16[288,1536]{1,0:T(8,128)(2,1)}, u32[]{:S(2)}, u32[]{:S(2)}) collective-permute-start(bf16[288,1536]{1,0:T(8,128)(2,1)} %bitcast.5.refs_0_), channel_id=1, source_target_pairs={{0,4},{2,6},{4,8},{6,10},{8,12},{10,14},{12,0},{14,2},{1,5},{3,7},... | collective-permute-start | bytes 2654216 | tf_op jit(solution)/shard_map/ppermute | solution.py:351
  2.2 1.7 %collective-permute-start.2 = (bf16[288,1536]{1,0:T(8,128)(2,1)}, bf16[288,1536]{1,0:T(8,128)(2,1)}, u32[]{:S(2)}, u32[]{:S(2)}) collective-permute-start(bf16[288,1536]{1,0:T(8,128)(2,1)} %bitcast.5.refs_0_), channel_id=1, source_target_pairs={{0,12},{2,14},{4,0},{6,2},{8,4},{10,6},{12,8},{14,10},{1,13},{3,15... | collective-permute-start | bytes 2654216 | tf_op jit(solution)/shard_map/ppermute | solution.py:351
  3.9 2.7 %fourier.1 = f32[256,128]{1,0:T(8,128)} custom-call(bf16[32,1440]{1,0:T(8,128)(2,1)} %bitcast.22, f32[32,1440]{1,0:T(8,128)} %bitcast.19, bf16[1440,512]{1,0:T(8,128)(2,1)} %constant.43.clone.table_ref), custom_call_target="tpu_custom_call" | custom-call | flops 235929600 | bytes 1882112 | tf_op jit(solution)/shard_map/fourier/pallas_call | solution.py:326
  6.7 8.1 %all-to-all-start = ((f32[16,16,128]{2,1,0:T(8,128)}), f32[16,16,128]{2,1,0:T(8,128)S(1)}, u32[]{:S(2)}, u32[]{:S(2)}) async-start(f32[16,16,128]{2,1,0:T(8,128)} %bitcast.18), calls=%async_computation | async-start | bytes 262144 | tf_op jit(solution)/shard_map/all_to_all | solution.py:380
  14.8 0.0 copy-start
  14.8 1.9 %copy-done = f32[16,128,384]{2,1,0:T(8,128)S(1)} copy-done((f32[16,128,384]{2,1,0:T(8,128)S(1)}, f32[16,128,384]{2,1,0:T(8,128)}, u32[]{:S(2)}) %copy-start) | copy-done | bytes 3145752
  16.7 0.2 cast.1.leg_ref
  16.8 0.8 copy-done.7
  17.6 0.1 copy.16
  17.7 0.1 reshape.42.own_ref
  17.7 4.6 %collective-permute-start = (bf16[64,1536]{1,0:T(8,128)(2,1)S(1)}, bf16[64,1536]{1,0:T(8,128)(2,1)S(1)}, u32[]{:S(2)}, u32[]{:S(2)}) collective-permute-start(bf16[64,1536]{1,0:T(8,128)(2,1)S(1)} %reshape.42.own_ref), channel_id=1, source_target_pairs={{0,2},{2,0},{4,6},{6,4},{8,10},{10,8},{12,14},{14,12},{1,3},{3,1},... | collective-permute-start | bytes 589832 | tf_op jit(solution)/shard_map/ppermute | solution.py:354
  22.3 0.0 all-to-all-done.spec_ref
  22.3 1.2 %legendre.1 = f32[16,8,640]{2,1,0:T(8,128)} custom-call(f32[16,16,128]{2,1,0:T(8,128)S(1)} %all-to-all-done.spec_ref, bf16[16,128,384]{2,1,0:T(8,128)(2,1)S(1)} %cast.1.leg_ref), custom_call_target="tpu_custom_call" | custom-call | flops 75497472 | bytes 2031616 | tf_op jit(solution)/shard_map/legendre/pallas_call | solution.py:326
  23.6 7.5 %all-to-all-start.1 = ((f32[16,8,640]{2,1,0:T(8,128)}), f32[16,8,640]{2,1,0:T(8,128)S(1)}, u32[]{:S(2)}, u32[]{:S(2)}) async-start(f32[16,8,640]{2,1,0:T(8,128)} %legendre.1), calls=%async_computation.1 | async-start | bytes 655360 | tf_op jit(solution)/shard_map/all_to_all | solution.py:410
  31.1 0.6 collective-permute-done.far_ref
  31.7 0.0 collective-permute-done.1.refs_1_
  31.7 0.0 collective-permute-done.2.refs_2_
  31.7 0.4 collective-permute-start.8
  32.1 2.7 %collective-permute-start.3 = (bf16[288,1536]{1,0:T(8,128)(2,1)}, bf16[288,1536]{1,0:T(8,128)(2,1)}, u32[]{:S(2)}, u32[]{:S(2)}) collective-permute-start(bf16[288,1536]{1,0:T(8,128)(2,1)} %bitcast.5.refs_0_), channel_id=1, source_target_pairs={{0,8},{2,10},{4,12},{6,14},{8,0},{10,2},{12,4},{14,6},{1,9},{3,11}... | collective-permute-start | bytes 2654216 | tf_op jit(solution)/shard_map/ppermute | solution.py:351
  35.4 4.1 %all-to-all-done.1.power_ref = f32[16,8,640]{2,1,0:T(8,128)S(1)} async-done(((f32[16,8,640]{2,1,0:T(8,128)}), f32[16,8,640]{2,1,0:T(8,128)S(1)}, u32[]{:S(2)}, u32[]{:S(2)}) %all-to-all-start.1) | async-done | bytes 327712 | tf_op jit(solution)/shard_map/all_to_all | solution.py:410
  39.6 2.6 %grad.1 = (f32[8,128]{1,0:T(8,128)S(1)}, f32[128,128]{1,0:T(8,128)}) custom-call(f32[16,8,640]{2,1,0:T(8,128)S(1)} %all-to-all-done.1.power_ref, f32[16,16,128]{2,1,0:T(8,128)S(1)} %all-to-all-done.spec_ref, bf16[16,128,384]{2,1,0:T(8,128)(2,1)S(1)} %cast.1.leg_ref), custom_call_target="tpu_custom_call" | custom-call | flops 125829120 | bytes 2101248 | tf_op jit(solution)/shard_map/grad/pallas_call | solution.py:326
  42.1 6.5 %all-to-all-start.2 = ((f32[16,8,128]{2,1,0:T(8,128)}), f32[16,8,128]{2,1,0:T(8,128)S(1)}, u32[]{:S(2)}, u32[]{:S(2)}) async-start(f32[16,8,128]{2,1,0:T(8,128)} %bitcast.7), calls=%async_computation.2 | async-start | bytes 131072 | tf_op jit(solution)/shard_map/all_to_all | solution.py:426
  48.6 0.0 copy-start.2
  48.6 0.1 collective-permute-start.4
  48.7 0.0 collective-permute-done.8.far_ref
  48.7 0.9 pair2.1.refs_8_
  49.6 1.8 %collective-permute-start.9 = (bf16[256,1536]{1,0:T(8,128)(2,1)}, bf16[256,1536]{1,0:T(8,128)(2,1)}, u32[]{:S(2)}, u32[]{:S(2)}) collective-permute-start(bf16[256,1536]{1,0:T(8,128)(2,1)} %pair2.1.refs_8_), channel_id=1, source_target_pairs={{0,8},{2,10},{4,12},{6,14},{8,0},{10,2},{12,4},{14,6},{1,9},{3,11}... | collective-permute-start | bytes 2359304 | tf_op jit(solution)/shard_map/ppermute | solution.py:351
  51.5 0.0 copy-done.1
  51.5 0.0 copy-done.2
  51.5 0.2 tables.1
  51.7 0.0 copy-start.8
  51.7 0.0 slice-start
  51.7 1.9 %all-to-all-done.2.band_ref = f32[16,8,128]{2,1,0:T(8,128)S(1)} async-done(((f32[16,8,128]{2,1,0:T(8,128)}), f32[16,8,128]{2,1,0:T(8,128)S(1)}, u32[]{:S(2)}, u32[]{:S(2)}) %all-to-all-start.2) | async-done | bytes 65568 | tf_op jit(solution)/shard_map/all_to_all | solution.py:426
  53.6 1.9 %field.1 = (f32[32,1440]{1,0:T(8,128)}, bf16[16,48,128]{2,1,0:T(8,128)(2,1)}) custom-call(s32[1]{0:T(128)} %copy.17.shift_ref, f32[16,8,128]{2,1,0:T(8,128)S(1)} %all-to-all-done.2.band_ref, bf16[512,1440]{1,0:T(8,128)(2,1)S(1)} %get-tuple-element.32.table, bf16[512,1536]{1,0:T(8,128)(2,1)S(1)} %get-tuple-element.33.cell), custom_call_target="tpu_custom_call" | custom-call | flops 235929600 | bytes 3493888 | tf_op jit(solution)/shard_map/field/pallas_call | solution.py:326
  55.6 7.1 %all-to-all-start.3 = ((bf16[16,48,128]{2,1,0:T(8,128)(2,1)}), bf16[16,48,128]{2,1,0:T(8,128)(2,1)S(1)}, u32[]{:S(2)}, u32[]{:S(2)}) async-start(bf16[16,48,128]{2,1,0:T(8,128)(2,1)} %get-tuple-element.35), calls=%async_computation.3 | async-start | bytes 393216 | tf_op jit(solution)/shard_map/all_to_all | solution.py:466
  62.7 0.0 copy-done.8
  62.7 0.6 reshape.46.gain_ref
  63.3 0.4 collective-permute-start.5
  63.7 0.1 collective-permute-start.6
  63.8 0.0 collective-permute-done.3.refs_3_
  63.8 0.4 collective-permute-start.7
  64.2 0.0 slice-done
  64.2 1.9 %fusion = bf16[2,48,1536]{2,1,0:T(8,128)(2,1)} fusion(s32[]{:T(128)S(6)} %select_n.16, bf16[2,360,1536]{2,1,0:T(8,128)(2,1)} %param.12, bf16[2,48,1536]{2,1,0:T(8,128)(2,1)S(1)} %slice-done), kind=kLoop, calls=%fused_computation.2 | loop fusion | flops 589824 | bytes 2801668 | tf_op jit(solution)/shard_map/concatenate | solution.py:464
  66.1 0.0 collective-permute-done.4.refs_4_
  66.1 0.1 collective-permute-start.10
  66.3 15.0 %all-to-all-done.3.cells_ref = bf16[16,48,128]{2,1,0:T(8,128)(2,1)S(1)} async-done(((bf16[16,48,128]{2,1,0:T(8,128)(2,1)}), bf16[16,48,128]{2,1,0:T(8,128)(2,1)S(1)}, u32[]{:S(2)}, u32[]{:S(2)}) %all-to-all-start.3) | async-done | bytes 196640 | tf_op jit(solution)/shard_map/all_to_all | solution.py:466
  81.3 0.0 collective-permute-done.9.refs_9_
  81.3 0.1 collective-permute-start.11
  81.4 0.0 collective-permute-done.5.refs_5_
  81.4 0.0 collective-permute-done.6.refs_6_
  81.4 0.0 copy-start.4
  81.4 0.0 collective-permute-done.7.refs_7_
  81.4 0.0 copy-start.5
  81.5 0.0 collective-permute-done.10.refs_10_
  81.5 2.5 %collective-permute-done.11.refs_11_ = bf16[256,1536]{1,0:T(8,128)(2,1)} collective-permute-done((bf16[256,1536]{1,0:T(8,128)(2,1)}, bf16[256,1536]{1,0:T(8,128)(2,1)}, u32[]{:S(2)}, u32[]{:S(2)}) %collective-permute-start.11) | collective-permute-done | bytes 786464 | tf_op jit(solution)/shard_map/ppermute | solution.py:357
  83.9 0.0 copy-done.6
  83.9 0.0 copy-done.3
  83.9 0.0 copy-done.4
  83.9 0.0 copy-done.5
  83.9 13.8 %attention.1 = bf16[1152,128]{1,0:T(8,128)(2,1)} custom-call(f32[1,1536]{1,0:T(1,128)} %reshape.46.gain_ref, bf16[16,48,128]{2,1,0:T(8,128)(2,1)} %copy-done.6, bf16[96,1536]{1,0:T(8,128)(2,1)} %bitcast.16, bf16[16,96,1536]{2,1,0:T(8,128)(2,1)} %proj_ref.1, bf16[288,1536]{1,0:T(8,128)(2,1)} %bitcast.5.refs_0_, ...), custom_call_target="tpu_custom_call" | custom-call | flops 1887436800 | bytes 15734784 | tf_op jit(solution)/shard_map/attention/pallas_call | solution.py:326
  97.8 7.0 %all-to-all-start.4 = ((bf16[16,72,128]{2,1,0:T(8,128)(2,1)}), bf16[16,72,128]{2,1,0:T(8,128)(2,1)S(1)}, u32[]{:S(2)}, u32[]{:S(2)}) async-start(bf16[16,72,128]{2,1,0:T(8,128)(2,1)} %bitcast.17), calls=%async_computation.4 | async-start | bytes 589824 | tf_op jit(solution)/shard_map/all_to_all | solution.py:487
  104.8 0.6 slice_reduce_fusion
  105.4 11.7 %all-to-all-done.4 = bf16[16,72,128]{2,1,0:T(8,128)(2,1)S(1)} async-done(((bf16[16,72,128]{2,1,0:T(8,128)(2,1)}), bf16[16,72,128]{2,1,0:T(8,128)(2,1)S(1)}, u32[]{:S(2)}, u32[]{:S(2)}) %all-to-all-start.4) | async-done | bytes 294944 | tf_op jit(solution)/shard_map/all_to_all | solution.py:487
  117.1 1.1 final.1
  (5 shorter events, 0.0 us)
Async XLA Ops:
  0.6 31.0 %collective-permute-start.1 = (bf16[288,1536]{1,0:T(8,128)(2,1)}, bf16[288,1536]{1,0:T(8,128)(2,1)}, u32[]{:S(2)}, u32[]{:S(2)}) collective-permute-start(bf16[288,1536]{1,0:T(8,128)(2,1)} %bitcast.5.refs_0_), channel_id=1, source_target_pairs={{0,4},{2,6},{4,8},{6,10},{8,12},{10,14},{12,0},{14,2},{1,5},{3,7},... | collective-permute-start | bytes 2654216 | tf_op jit(solution)/shard_map/ppermute | solution.py:351
  2.2 29.5 %collective-permute-start.2 = (bf16[288,1536]{1,0:T(8,128)(2,1)}, bf16[288,1536]{1,0:T(8,128)(2,1)}, u32[]{:S(2)}, u32[]{:S(2)}) collective-permute-start(bf16[288,1536]{1,0:T(8,128)(2,1)} %bitcast.5.refs_0_), channel_id=1, source_target_pairs={{0,12},{2,14},{4,0},{6,2},{8,4},{10,6},{12,8},{14,10},{1,13},{3,15... | collective-permute-start | bytes 2654216 | tf_op jit(solution)/shard_map/ppermute | solution.py:351
  6.7 15.6 %all-to-all-start = ((f32[16,16,128]{2,1,0:T(8,128)}), f32[16,16,128]{2,1,0:T(8,128)S(1)}, u32[]{:S(2)}, u32[]{:S(2)}) async-start(f32[16,16,128]{2,1,0:T(8,128)} %bitcast.18), calls=%async_computation | async-start | bytes 262144 | tf_op jit(solution)/shard_map/all_to_all | solution.py:380
  14.8 1.9 %copy-start = (f32[16,128,384]{2,1,0:T(8,128)S(1)}, f32[16,128,384]{2,1,0:T(8,128)}, u32[]{:S(2)}) copy-start(f32[16,128,384]{2,1,0:T(8,128)} %leg_ref) | copy-start | bytes 9437188
  16.7 0.9 copy-start.7
  17.7 13.9 %collective-permute-start = (bf16[64,1536]{1,0:T(8,128)(2,1)S(1)}, bf16[64,1536]{1,0:T(8,128)(2,1)S(1)}, u32[]{:S(2)}, u32[]{:S(2)}) collective-permute-start(bf16[64,1536]{1,0:T(8,128)(2,1)S(1)} %reshape.42.own_ref), channel_id=1, source_target_pairs={{0,2},{2,0},{4,6},{6,4},{8,10},{10,8},{12,14},{14,12},{1,3},{3,1},... | collective-permute-start | bytes 589832 | tf_op jit(solution)/shard_map/ppermute | solution.py:354
  23.6 16.0 %all-to-all-start.1 = ((f32[16,8,640]{2,1,0:T(8,128)}), f32[16,8,640]{2,1,0:T(8,128)S(1)}, u32[]{:S(2)}, u32[]{:S(2)}) async-start(f32[16,8,640]{2,1,0:T(8,128)} %legendre.1), calls=%async_computation.1 | async-start | bytes 655360 | tf_op jit(solution)/shard_map/all_to_all | solution.py:410
  31.7 17.0 %collective-permute-start.8 = (bf16[128,1536]{1,0:T(8,128)(2,1)S(1)}, bf16[128,1536]{1,0:T(8,128)(2,1)S(1)}, u32[]{:S(2)}, u32[]{:S(2)}) collective-permute-start(bf16[128,1536]{1,0:T(8,128)(2,1)S(1)} %pair.1.own_ref), channel_id=1, source_target_pairs={{0,4},{2,6},{4,0},{6,2},{8,12},{10,14},{12,8},{14,10},{1,5},{3,7},... | collective-permute-start | bytes 1179656 | tf_op jit(solution)/shard_map/ppermute | solution.py:408
  32.1 31.8 %collective-permute-start.3 = (bf16[288,1536]{1,0:T(8,128)(2,1)}, bf16[288,1536]{1,0:T(8,128)(2,1)}, u32[]{:S(2)}, u32[]{:S(2)}) collective-permute-start(bf16[288,1536]{1,0:T(8,128)(2,1)} %bitcast.5.refs_0_), channel_id=1, source_target_pairs={{0,8},{2,10},{4,12},{6,14},{8,0},{10,2},{12,4},{14,6},{1,9},{3,11}... | collective-permute-start | bytes 2654216 | tf_op jit(solution)/shard_map/ppermute | solution.py:351
  42.1 11.5 %all-to-all-start.2 = ((f32[16,8,128]{2,1,0:T(8,128)}), f32[16,8,128]{2,1,0:T(8,128)S(1)}, u32[]{:S(2)}, u32[]{:S(2)}) async-start(f32[16,8,128]{2,1,0:T(8,128)} %bitcast.7), calls=%async_computation.2 | async-start | bytes 131072 | tf_op jit(solution)/shard_map/all_to_all | solution.py:426
  48.6 2.9 %copy-start.1 = (bf16[512,1440]{1,0:T(8,128)(2,1)S(1)}, bf16[512,1440]{1,0:T(8,128)(2,1)}, u32[]{:S(2)}) copy-start(bf16[512,1440]{1,0:T(8,128)(2,1)} %constant.44.clone.table_ref) | copy-start | bytes 4423684
  48.6 2.9 %copy-start.2 = (bf16[512,1536]{1,0:T(8,128)(2,1)S(1)}, bf16[512,1536]{1,0:T(8,128)(2,1)}, u32[]{:S(2)}) copy-start(bf16[512,1536]{1,0:T(8,128)(2,1)} %constant.45.clone.cell_ref) | copy-start | bytes 4718596
  48.6 17.5 %collective-permute-start.4 = (bf16[288,1536]{1,0:T(8,128)(2,1)}, bf16[288,1536]{1,0:T(8,128)(2,1)}, u32[]{:S(2)}, u32[]{:S(2)}) collective-permute-start(bf16[288,1536]{1,0:T(8,128)(2,1)} %bitcast.5.refs_0_), channel_id=1, source_target_pairs={{0,1},{1,0},{2,3},{3,2},{4,5},{5,4},{6,7},{7,6},{8,9},{9,8},{10,11... | collective-permute-start | bytes 2654216 | tf_op jit(solution)/shard_map/ppermute | solution.py:357
  49.6 31.6 %collective-permute-start.9 = (bf16[256,1536]{1,0:T(8,128)(2,1)}, bf16[256,1536]{1,0:T(8,128)(2,1)}, u32[]{:S(2)}, u32[]{:S(2)}) collective-permute-start(bf16[256,1536]{1,0:T(8,128)(2,1)} %pair2.1.refs_8_), channel_id=1, source_target_pairs={{0,8},{2,10},{4,12},{6,14},{8,0},{10,2},{12,4},{14,6},{1,9},{3,11}... | collective-permute-start | bytes 2359304 | tf_op jit(solution)/shard_map/ppermute | solution.py:351
  51.7 11.0 %copy-start.8 = (f32[1536]{0:T(1024)S(1)}, f32[1536]{0:T(1024)}, u32[]{:S(2)}) copy-start(f32[1536]{0:T(1024)} %param.16) | copy-start | bytes 18436
  51.7 12.5 %slice-start = ((bf16[2,360,1536]{2,1,0:T(8,128)(2,1)}), bf16[2,48,1536]{2,1,0:T(8,128)(2,1)S(1)}, s32[]{:S(2)}) async-start(bf16[2,360,1536]{2,1,0:T(8,128)(2,1)} %param.12), calls=%async_computation.5 | async-start | bytes 589824 | tf_op jit(solution)/shard_map/slice | solution.py:464
  55.6 25.7 %all-to-all-start.3 = ((bf16[16,48,128]{2,1,0:T(8,128)(2,1)}), bf16[16,48,128]{2,1,0:T(8,128)(2,1)S(1)}, u32[]{:S(2)}, u32[]{:S(2)}) async-start(bf16[16,48,128]{2,1,0:T(8,128)(2,1)} %get-tuple-element.35), calls=%async_computation.3 | async-start | bytes 393216 | tf_op jit(solution)/shard_map/all_to_all | solution.py:466
  63.3 18.1 %collective-permute-start.5 = (bf16[288,1536]{1,0:T(8,128)(2,1)}, bf16[288,1536]{1,0:T(8,128)(2,1)S(1)}, u32[]{:S(2)}, u32[]{:S(2)}) collective-permute-start(bf16[288,1536]{1,0:T(8,128)(2,1)} %collective-permute-done.1.refs_1_), channel_id=1, source_target_pairs={{0,1},{1,0},{2,3},{3,2},{4,5},{5,4},{6,7},{7,6},{8,9},{9,8},{10,11... | collective-permute-start | bytes 2654216 | tf_op jit(solution)/shard_map/ppermute | solution.py:357
  63.7 17.7 %collective-permute-start.6 = (bf16[288,1536]{1,0:T(8,128)(2,1)}, bf16[288,1536]{1,0:T(8,128)(2,1)S(1)}, u32[]{:S(2)}, u32[]{:S(2)}) collective-permute-start(bf16[288,1536]{1,0:T(8,128)(2,1)} %collective-permute-done.2.refs_2_), channel_id=1, source_target_pairs={{0,1},{1,0},{2,3},{3,2},{4,5},{5,4},{6,7},{7,6},{8,9},{9,8},{10,11... | collective-permute-start | bytes 2654216 | tf_op jit(solution)/shard_map/ppermute | solution.py:357
  63.8 17.6 %collective-permute-start.7 = (bf16[288,1536]{1,0:T(8,128)(2,1)}, bf16[288,1536]{1,0:T(8,128)(2,1)S(1)}, u32[]{:S(2)}, u32[]{:S(2)}) collective-permute-start(bf16[288,1536]{1,0:T(8,128)(2,1)} %collective-permute-done.3.refs_3_), channel_id=1, source_target_pairs={{0,1},{1,0},{2,3},{3,2},{4,5},{5,4},{6,7},{7,6},{8,9},{9,8},{10,11... | collective-permute-start | bytes 2654216 | tf_op jit(solution)/shard_map/ppermute | solution.py:357
  66.1 15.3 %collective-permute-start.10 = (bf16[256,1536]{1,0:T(8,128)(2,1)}, bf16[256,1536]{1,0:T(8,128)(2,1)}, u32[]{:S(2)}, u32[]{:S(2)}) collective-permute-start(bf16[256,1536]{1,0:T(8,128)(2,1)} %pair2.1.refs_8_), channel_id=1, source_target_pairs={{0,1},{1,0},{2,3},{3,2},{4,5},{5,4},{6,7},{7,6},{8,9},{9,8},{10,11... | collective-permute-start | bytes 2359304 | tf_op jit(solution)/shard_map/ppermute | solution.py:357
  81.3 2.6 %copy-start.6 = (bf16[16,48,128]{2,1,0:T(8,128)(2,1)}, bf16[16,48,128]{2,1,0:T(8,128)(2,1)S(1)}, u32[]{:S(2)}) copy-start(bf16[16,48,128]{2,1,0:T(8,128)(2,1)S(1)} %all-to-all-done.3.cells_ref) | copy-start | bytes 589828
  81.3 2.6 %collective-permute-start.11 = (bf16[256,1536]{1,0:T(8,128)(2,1)}, bf16[256,1536]{1,0:T(8,128)(2,1)}, u32[]{:S(2)}, u32[]{:S(2)}) collective-permute-start(bf16[256,1536]{1,0:T(8,128)(2,1)} %collective-permute-done.9.refs_9_), channel_id=1, source_target_pairs={{0,1},{1,0},{2,3},{3,2},{4,5},{5,4},{6,7},{7,6},{8,9},{9,8},{10,11... | collective-permute-start | bytes 2359304 | tf_op jit(solution)/shard_map/ppermute | solution.py:357
  81.4 2.5 %copy-start.3 = (bf16[288,1536]{1,0:T(8,128)(2,1)}, bf16[288,1536]{1,0:T(8,128)(2,1)S(1)}, u32[]{:S(2)}) copy-start(bf16[288,1536]{1,0:T(8,128)(2,1)S(1)} %collective-permute-done.5.refs_5_) | copy-start | bytes 2654212
  81.4 2.5 %copy-start.4 = (bf16[288,1536]{1,0:T(8,128)(2,1)}, bf16[288,1536]{1,0:T(8,128)(2,1)S(1)}, u32[]{:S(2)}) copy-start(bf16[288,1536]{1,0:T(8,128)(2,1)S(1)} %collective-permute-done.6.refs_6_) | copy-start | bytes 2654212
  81.4 2.5 %copy-start.5 = (bf16[288,1536]{1,0:T(8,128)(2,1)}, bf16[288,1536]{1,0:T(8,128)(2,1)S(1)}, u32[]{:S(2)}) copy-start(bf16[288,1536]{1,0:T(8,128)(2,1)S(1)} %collective-permute-done.7.refs_7_) | copy-start | bytes 2654212
  97.8 19.4 %all-to-all-start.4 = ((bf16[16,72,128]{2,1,0:T(8,128)(2,1)}), bf16[16,72,128]{2,1,0:T(8,128)(2,1)S(1)}, u32[]{:S(2)}, u32[]{:S(2)}) async-start(bf16[16,72,128]{2,1,0:T(8,128)(2,1)} %bitcast.17), calls=%async_computation.4 | async-start | bytes 589824 | tf_op jit(solution)/shard_map/all_to_all | solution.py:487

commit v3 on v2

--- a/solution.py
+++ b/solution.py
@@ -209,8 +209,8 @@
 
 
 def attention_kernel(gain_ref, cells_ref, tok_ref, proj_ref, *refs):
-    w_refs, d_refs, out_ref = refs[:8], refs[8:12], refs[12]
-    got, tok, decoder, proj, w, sems = refs[13:]
+    w_refs, d_refs, out_ref = refs[:8], refs[8:16], refs[16]
+    got, tok, decoder, proj, w, sems = refs[17:]
     place, core = lax.axis_index("loss"), lax.axis_index("vars")
     x_at, z_at = place // 2, place % 2
     places = [((x_at + dx) % 4, c) for c in (core, 1 - core) for dx in (0, 3, 1, 2)]
@@ -240,7 +240,7 @@
             both = dot_nt(w[b * 288 : b * 288 + 576], norm_out).astype(bf16)
         if b == 4:
             d_copies = fetch(
-                [(d_refs[i], decoder.at[pl.ds(i * 256, 256)]) for i in range(4)], sems.at[2]
+                [(d_refs[i], decoder.at[pl.ds(i * 128, 128)]) for i in range(8)], sems.at[2]
             )
             p_copies = fetch(
                 [
@@ -257,7 +257,7 @@
         heads.append((q, k, values, a / jnp.sum(a, axis=0, keepdims=True)))
     first[1].wait()
     rows = [[], []]
-    for x_from, c_from in [(x_at ^ k, c) for c in (core, 1 - core) for k in range(4)]:
+    for x_from, c_from in places:
         near = got[(x_from * 2 + z_at) * 2 + c_from].astype(f32)
         far = got[(x_from * 2 + 1 - z_at) * 2 + c_from].astype(f32)
         for r in range(2):
@@ -405,7 +405,7 @@
         flops=BUSY,
         name="pair",
     )
-    d_far = lax.ppermute(d_own, "loss", [(i, i ^ 2) for i in range(8)])
+    d_all = [d_own, along_x(d_own, 1), along_x(d_own, 3), along_x(d_own, 2)]
     w_all += [across(after(w, d_own)) for w in w_all[:3]]
     powers = lax.all_to_all(powers, "proc", 0, 0, tiled=True)
     amse, grad_spectra = call(
@@ -430,21 +430,13 @@
         [shape((512, LON), bf16), shape((512, 4 * PAD), bf16)],
         [],
         [],
-        [after(grad_spectra, w_all[1:3]), back, cells],
+        [after(grad_spectra, d_all[1:3]), back, cells],
         scratch=[pltpu.SemaphoreType.DMA((2,))],
         flops=BUSY,
         name="tables",
     )
-    d_own = call(
-        pair_kernel,
-        shape((256, D), bf16),
-        [],
-        [*after((d_own, d_far), grad_spectra)],
-        flops=BUSY,
-        name="pair2",
-    )
-    d_far = along_x(d_own, 2)
-    d_all = [d_own, d_far, across(after(d_own, (back, w_all[4])))]
+    d_all.append(across(after(d_own, (back, w_all[4]))))
+    d_all += [across(after(d, back)) for d in d_all[1:3]]
     field_grad, cell_grads = call(
         field_kernel,
         [shape((32, LON)), shape((16, GROUP, 128), bf16)],
@@ -459,13 +451,13 @@
         name="field",
         spaces=[HBM, VMEM],
     )
-    w_all.append(across(after(w_all[3], cell_grads)))
     own_tokens = after(tokens, cell_grads)
     own_tokens = jnp.concatenate([own_tokens, own_tokens[:, :GROUP]], axis=1)
     own_tokens = lax.dynamic_slice_in_dim(own_tokens, start, GROUP, 1).reshape(TOK, D)
     cell_grads = lax.all_to_all(cell_grads, group, 0, 0, tiled=True)
     gain = ln_gain.reshape(1, D)
-    d_all.append(across(after(d_far, (cell_grads, own_tokens, gain))))
+    w_all.append(across(after(w_all[3], (cell_grads, own_tokens, gain))))
+    d_all.append(across(after(d_all[3], (cell_grads, own_tokens, gain))))
     parts = call(
         attention_kernel,
         shape((16 * 72, 128), bf16),

time: 119 us -> 134 us (1.13)
  local copies, waits for them, and re-layouts: 4.03 us -> 11.3 us
  waiting for transfers between devices: 35.7 us -> 40.5 us
  starting transfers between devices: 50.3 us -> 54 us
    ppermute x4 -> x6, waiting for transfers between devices: 0.01 us -> 17.6 us  [along_x(): return lax.ppermute(block, 'loss', pairs)]
    all_to_all x1, waiting for transfers between devices: 15 us -> 3.95 us  [body(): cell_grads = lax.all_to_all(cell_grads, group, 0, 0, tiled=True)]
    unnamed x18 -> x32, local copies, waits for them, and re-layouts: 2.67 us -> 9 us
    ppermute x4 -> x6, starting transfers between devices: 7.85 us -> 10.7 us  [along_x(): return lax.ppermute(block, 'loss', pairs)]
    all_to_all x1, waiting for transfers between devices: 1.87 us -> 0.01 us  [body(): lax.all_to_all(grad_spectra.reshape(16, 8, 128), 'proc', 0, 0, tiled=True)]
    ppermute x6 -> x8, waiting for transfers between devices: 2.47 us -> 3.41 us  [across(): return lax.ppermute(block, 'vars', [(0, 1), (1, 0)])]
    pallas_call x10 -> x9, Pallas kernels: 24.8 us -> 24 us  [call(): pl.pallas_call(kernel, out_shape=outs, in_specs=[SMEM] * len(scalars) + [...]
  transfers between devices with their start and end apart: 17 -> 20, of which waited for: 6 -> 10; matrix products, arithmetic and copies ran while one was open for 3% -> 3% of each run, Pallas kernels for 8% -> 7%
where the time goes in v3:
time: 134 us; the launch traced here: 133 us
  starting transfers between devices  54 us (40%)
  waiting for transfers between devices  40.5 us (30%)
  Pallas kernels  24 us (18%)
  local copies, waits for them, and re-layouts  11.3 us (8%)
  other arithmetic  1.9 us (1%)
  between operations  1.47 us (1%)
    pallas_call x9, Pallas kernels, call(): pl.pallas_call(kernel, out_shape=outs, in_specs=[SMEM] * len(scalars) + [...  24 us
    ppermute x6, waiting for transfers between devices, along_x(): return lax.ppermute(block, 'loss', pairs)  17.6 us
    all_to_all x1, waiting for transfers between devices, body(): parts = lax.all_to_all(parts.reshape(16, 72, 128), group, 0, 0, tiled=True)  11.7 us
    ppermute x6, starting transfers between devices, along_x(): return lax.ppermute(block, 'loss', pairs)  10.7 us
    unnamed x32, local copies, waits for them, and re-layouts  9 us
    all_to_all x1, starting transfers between devices, body(): lax.all_to_all(spectra.reshape(16, 16, 128), 'proc', 0, 0, tiled=True)  8.1 us
    all_to_all x1, starting transfers between devices, body(): cell_grads = lax.all_to_all(cell_grads, group, 0, 0, tiled=True)  7.61 us
    all_to_all x1, starting transfers between devices, body(): powers = lax.all_to_all(powers, 'proc', 0, 0, tiled=True)  7.52 us
  transfers between devices with their start and end apart: 20, of which 10 were waited for; matrix products, arithmetic and copies ran while one was open for 3% of the time, Pallas kernels for 7%

profile of v3, /device:TPU:72, one launch (start us, length us, event | category | flops | bytes accessed | tf_op | source)
XLA Modules:
  0.0 133.2 jit_solution(8896849357833467619)
XLA Ops:
  0.6 1.6 %collective-permute-start.1 = (bf16[288,1536]{1,0:T(8,128)(2,1)}, bf16[288,1536]{1,0:T(8,128)(2,1)}, u32[]{:S(2)}, u32[]{:S(2)}) collective-permute-start(bf16[288,1536]{1,0:T(8,128)(2,1)} %bitcast.5.refs_0_), channel_id=1, source_target_pairs={{0,4},{2,6},{4,8},{6,10},{8,12},{10,14},{12,0},{14,2},{1,5},{3,7},... | collective-permute-start | bytes 2654216 | tf_op jit(solution)/shard_map/ppermute | solution.py:351
  2.2 1.7 %collective-permute-start.2 = (bf16[288,1536]{1,0:T(8,128)(2,1)}, bf16[288,1536]{1,0:T(8,128)(2,1)}, u32[]{:S(2)}, u32[]{:S(2)}) collective-permute-start(bf16[288,1536]{1,0:T(8,128)(2,1)} %bitcast.5.refs_0_), channel_id=1, source_target_pairs={{0,12},{2,14},{4,0},{6,2},{8,4},{10,6},{12,8},{14,10},{1,13},{3,15... | collective-permute-start | bytes 2654216 | tf_op jit(solution)/shard_map/ppermute | solution.py:351
  3.9 2.7 %fourier.1 = f32[256,128]{1,0:T(8,128)} custom-call(bf16[32,1440]{1,0:T(8,128)(2,1)} %bitcast.22, f32[32,1440]{1,0:T(8,128)} %bitcast.19, bf16[1440,512]{1,0:T(8,128)(2,1)} %constant.43.clone.table_ref), custom_call_target="tpu_custom_call" | custom-call | flops 235929600 | bytes 1882112 | tf_op jit(solution)/shard_map/fourier/pallas_call | solution.py:326
  6.7 8.1 %all-to-all-start = ((f32[16,16,128]{2,1,0:T(8,128)}), f32[16,16,128]{2,1,0:T(8,128)S(1)}, u32[]{:S(2)}, u32[]{:S(2)}) async-start(f32[16,16,128]{2,1,0:T(8,128)} %bitcast.18), calls=%async_computation | async-start | bytes 262144 | tf_op jit(solution)/shard_map/all_to_all | solution.py:380
  14.8 1.9 %copy-done.2 = f32[16,128,384]{2,1,0:T(8,128)S(1)} copy-done((f32[16,128,384]{2,1,0:T(8,128)S(1)}, f32[16,128,384]{2,1,0:T(8,128)}, u32[]{:S(2)}) %copy-start.2) | copy-done | bytes 3145752
  16.7 0.2 cast.1.leg_ref
  16.8 0.8 copy-done.14
  17.6 0.1 copy.16
  17.7 0.1 reshape.42.own_ref
  17.7 4.6 %collective-permute-start = (bf16[64,1536]{1,0:T(8,128)(2,1)S(1)}, bf16[64,1536]{1,0:T(8,128)(2,1)S(1)}, u32[]{:S(2)}, u32[]{:S(2)}) collective-permute-start(bf16[64,1536]{1,0:T(8,128)(2,1)S(1)} %reshape.42.own_ref), channel_id=1, source_target_pairs={{0,2},{2,0},{4,6},{6,4},{8,10},{10,8},{12,14},{14,12},{1,3},{3,1},... | collective-permute-start | bytes 589832 | tf_op jit(solution)/shard_map/ppermute | solution.py:354
  22.3 0.0 all-to-all-done.spec_ref
  22.3 1.3 legendre.1
  23.6 7.5 %all-to-all-start.1 = ((f32[16,8,640]{2,1,0:T(8,128)}), f32[16,8,640]{2,1,0:T(8,128)S(1)}, u32[]{:S(2)}, u32[]{:S(2)}) async-start(f32[16,8,640]{2,1,0:T(8,128)} %legendre.1), calls=%async_computation.1 | async-start | bytes 655360 | tf_op jit(solution)/shard_map/all_to_all | solution.py:410
  31.1 0.6 collective-permute-done.far_ref
  31.7 0.0 collective-permute-done.1.refs_1_
  31.7 0.0 collective-permute-done.2.refs_2_
  31.7 0.4 collective-permute-start.3
  32.1 3.0 %collective-permute-start.4 = (bf16[128,1536]{1,0:T(8,128)(2,1)S(1)}, bf16[128,1536]{1,0:T(8,128)(2,1)}, u32[]{:S(2)}, u32[]{:S(2)}) collective-permute-start(bf16[128,1536]{1,0:T(8,128)(2,1)S(1)} %pair.1.refs_8_), channel_id=1, source_target_pairs={{0,12},{2,14},{4,0},{6,2},{8,4},{10,6},{12,8},{14,10},{1,13},{3,15... | collective-permute-start | bytes 1179656 | tf_op jit(solution)/shard_map/ppermute | solution.py:351
  35.0 0.6 collective-permute-start.5
  36.3 3.3 %all-to-all-done.1.power_ref = f32[16,8,640]{2,1,0:T(8,128)S(1)} async-done(((f32[16,8,640]{2,1,0:T(8,128)}), f32[16,8,640]{2,1,0:T(8,128)S(1)}, u32[]{:S(2)}, u32[]{:S(2)}) %all-to-all-start.1) | async-done | bytes 327712 | tf_op jit(solution)/shard_map/all_to_all | solution.py:410
  39.6 2.6 %grad.1 = (f32[8,128]{1,0:T(8,128)S(1)}, f32[128,128]{1,0:T(8,128)}) custom-call(f32[16,8,640]{2,1,0:T(8,128)S(1)} %all-to-all-done.1.power_ref, f32[16,16,128]{2,1,0:T(8,128)S(1)} %all-to-all-done.spec_ref, bf16[16,128,384]{2,1,0:T(8,128)(2,1)S(1)} %cast.1.leg_ref), custom_call_target="tpu_custom_call" | custom-call | flops 125829120 | bytes 2101248 | tf_op jit(solution)/shard_map/grad/pallas_call | solution.py:326
  42.1 6.9 %all-to-all-start.2 = ((f32[16,8,128]{2,1,0:T(8,128)}), f32[16,8,128]{2,1,0:T(8,128)}, u32[]{:S(2)}, u32[]{:S(2)}) async-start(f32[16,8,128]{2,1,0:T(8,128)} %bitcast.7), calls=%async_computation.2 | async-start | bytes 131072 | tf_op jit(solution)/shard_map/all_to_all | solution.py:426
  49.0 0.0 collective-permute-start.6
  49.0 13.8 %collective-permute-done.3.refs_9_ = bf16[128,1536]{1,0:T(8,128)(2,1)S(1)} collective-permute-done((bf16[128,1536]{1,0:T(8,128)(2,1)S(1)}, bf16[128,1536]{1,0:T(8,128)(2,1)S(1)}, u32[]{:S(2)}, u32[]{:S(2)}) %collective-permute-start.3) | collective-permute-done | bytes 393248 | tf_op jit(solution)/shard_map/ppermute | solution.py:351
  62.7 0.8 copy-done.9
  63.5 0.0 collective-permute-done.4.refs_10_
  63.5 1.4 %copy-done.3 = bf16[512,1440]{1,0:T(8,128)(2,1)S(1)} copy-done((bf16[512,1440]{1,0:T(8,128)(2,1)S(1)}, bf16[512,1440]{1,0:T(8,128)(2,1)}, u32[]{:S(2)}) %copy-start.3) | copy-done | bytes 1474584
  64.9 1.4 %copy-done.4 = bf16[512,1536]{1,0:T(8,128)(2,1)S(1)} copy-done((bf16[512,1536]{1,0:T(8,128)(2,1)S(1)}, bf16[512,1536]{1,0:T(8,128)(2,1)}, u32[]{:S(2)}) %copy-start.4) | copy-done | bytes 1572888
  66.3 0.2 tables.1
  66.6 0.0 copy-start.15
  66.6 0.0 all-to-all-done.2.band_ref
  66.6 2.1 %field.1 = (f32[32,1440]{1,0:T(8,128)}, bf16[16,48,128]{2,1,0:T(8,128)(2,1)S(1)}) custom-call(s32[1]{0:T(128)} %copy.17.shift_ref, f32[16,8,128]{2,1,0:T(8,128)} %all-to-all-done.2.band_ref, bf16[512,1440]{1,0:T(8,128)(2,1)S(1)} %get-tuple-element.32.table, bf16[512,1536]{1,0:T(8,128)(2,1)S(1)} %get-tuple-element.33.cell), custom_call_target="tpu_custom_call" | custom-call | flops 235929600 | bytes 3493888 | tf_op jit(solution)/shard_map/field/pallas_call | solution.py:326
  68.7 0.7 copy-done.1
  69.4 7.6 %all-to-all-start.3 = ((bf16[16,48,128]{2,1,0:T(8,128)(2,1)}), bf16[16,48,128]{2,1,0:T(8,128)(2,1)S(1)}, u32[]{:S(2)}, u32[]{:S(2)}) async-start(bf16[16,48,128]{2,1,0:T(8,128)(2,1)} %copy-done.1), calls=%async_computation.3 | async-start | bytes 393216 | tf_op jit(solution)/shard_map/all_to_all | solution.py:457
  77.0 3.4 %collective-permute-start.10 = (bf16[128,1536]{1,0:T(8,128)(2,1)S(1)}, bf16[128,1536]{1,0:T(8,128)(2,1)}, u32[]{:S(2)}, u32[]{:S(2)}) collective-permute-start(bf16[128,1536]{1,0:T(8,128)(2,1)S(1)} %pair.1.refs_8_), channel_id=1, source_target_pairs={{0,8},{2,10},{4,12},{6,14},{8,0},{10,2},{12,4},{14,6},{1,9},{3,11}... | collective-permute-start | bytes 1179656 | tf_op jit(solution)/shard_map/ppermute | solution.py:351
  80.4 0.6 reshape.46.gain_ref
  81.0 0.0 collective-permute-start.7
  81.0 0.5 collective-permute-start.8
  81.5 1.0 slice.7
  82.5 1.9 %fusion = bf16[2,48,1536]{2,1,0:T(8,128)(2,1)} fusion(s32[]{:T(128)S(6)} %select_n.16, bf16[2,360,1536]{2,1,0:T(8,128)(2,1)} %param.12, bf16[2,48,1536]{2,1,0:T(8,128)(2,1)S(1)} %slice.7), kind=kLoop, calls=%fused_computation.2 | loop fusion | flops 589824 | bytes 2801668 | tf_op jit(solution)/shard_map/concatenate | solution.py:455
  84.4 0.0 collective-permute-done.5.refs_3_
  84.4 3.9 %all-to-all-done.3.cells_ref = bf16[16,48,128]{2,1,0:T(8,128)(2,1)S(1)} async-done(((bf16[16,48,128]{2,1,0:T(8,128)(2,1)}), bf16[16,48,128]{2,1,0:T(8,128)(2,1)S(1)}, u32[]{:S(2)}, u32[]{:S(2)}) %all-to-all-start.3) | async-done | bytes 196640 | tf_op jit(solution)/shard_map/all_to_all | solution.py:457
  88.4 0.0 collective-permute-start.9
  88.4 3.9 %collective-permute-done.10.refs_11_ = bf16[128,1536]{1,0:T(8,128)(2,1)} collective-permute-done((bf16[128,1536]{1,0:T(8,128)(2,1)S(1)}, bf16[128,1536]{1,0:T(8,128)(2,1)}, u32[]{:S(2)}, u32[]{:S(2)}) %collective-permute-start.10) | collective-permute-done | bytes 393248 | tf_op jit(solution)/shard_map/ppermute | solution.py:351
  92.3 0.0 collective-permute-start.12
  92.3 0.0 collective-permute-done.6.refs_4_
  92.3 0.5 collective-permute-start.13
  92.8 1.4 %collective-permute-done.12.refs_13_ = bf16[128,1536]{1,0:T(8,128)(2,1)S(1)} collective-permute-done((bf16[128,1536]{1,0:T(8,128)(2,1)}, bf16[128,1536]{1,0:T(8,128)(2,1)S(1)}, u32[]{:S(2)}, u32[]{:S(2)}) %collective-permute-start.12) | collective-permute-done | bytes 393248 | tf_op jit(solution)/shard_map/ppermute | solution.py:357
  94.2 0.1 collective-permute-start.14
  94.3 0.4 collective-permute-done.13.refs_14_
  94.8 0.1 collective-permute-start.11
  94.9 0.0 collective-permute-done.7.refs_5_
  94.9 0.0 collective-permute-done.8.refs_6_
  94.9 1.2 collective-permute-done.14.refs_15_
  96.1 0.4 collective-permute-done.11.refs_12_
  96.5 0.4 copy-done.12
  96.9 0.8 copy-done.13
  97.7 0.0 collective-permute-done.9.refs_7_
  97.7 0.9 copy-done.7
  98.6 13.8 %attention.1 = bf16[1152,128]{1,0:T(8,128)(2,1)} custom-call(f32[1,1536]{1,0:T(1,128)} %reshape.46.gain_ref, bf16[16,48,128]{2,1,0:T(8,128)(2,1)} %copy-done.8, bf16[96,1536]{1,0:T(8,128)(2,1)} %bitcast.16, bf16[16,96,1536]{2,1,0:T(8,128)(2,1)} %proj_ref.1, bf16[288,1536]{1,0:T(8,128)(2,1)} %bitcast.5.refs_0_, ...), custom_call_target="tpu_custom_call" | custom-call | flops 1887436800 | bytes 15734784 | tf_op jit(solution)/shard_map/attention/pallas_call | solution.py:326
  112.4 7.4 %all-to-all-start.4 = ((bf16[16,72,128]{2,1,0:T(8,128)(2,1)}), bf16[16,72,128]{2,1,0:T(8,128)(2,1)S(1)}, u32[]{:S(2)}, u32[]{:S(2)}) async-start(bf16[16,72,128]{2,1,0:T(8,128)(2,1)} %bitcast.17), calls=%async_computation.4 | async-start | bytes 589824 | tf_op jit(solution)/shard_map/all_to_all | solution.py:479
  119.8 0.6 slice_reduce_fusion
  120.4 11.7 %all-to-all-done.4 = bf16[16,72,128]{2,1,0:T(8,128)(2,1)S(1)} async-done(((bf16[16,72,128]{2,1,0:T(8,128)(2,1)}), bf16[16,72,128]{2,1,0:T(8,128)(2,1)S(1)}, u32[]{:S(2)}, u32[]{:S(2)}) %all-to-all-start.4) | async-done | bytes 294944 | tf_op jit(solution)/shard_map/all_to_all | solution.py:479
  132.1 1.1 final.1
  (23 shorter events, 0.1 us)
Async XLA Ops:
  0.6 31.0 %collective-permute-start.1 = (bf16[288,1536]{1,0:T(8,128)(2,1)}, bf16[288,1536]{1,0:T(8,128)(2,1)}, u32[]{:S(2)}, u32[]{:S(2)}) collective-permute-start(bf16[288,1536]{1,0:T(8,128)(2,1)} %bitcast.5.refs_0_), channel_id=1, source_target_pairs={{0,4},{2,6},{4,8},{6,10},{8,12},{10,14},{12,0},{14,2},{1,5},{3,7},... | collective-permute-start | bytes 2654216 | tf_op jit(solution)/shard_map/ppermute | solution.py:351
  2.2 29.5 %collective-permute-start.2 = (bf16[288,1536]{1,0:T(8,128)(2,1)}, bf16[288,1536]{1,0:T(8,128)(2,1)}, u32[]{:S(2)}, u32[]{:S(2)}) collective-permute-start(bf16[288,1536]{1,0:T(8,128)(2,1)} %bitcast.5.refs_0_), channel_id=1, source_target_pairs={{0,12},{2,14},{4,0},{6,2},{8,4},{10,6},{12,8},{14,10},{1,13},{3,15... | collective-permute-start | bytes 2654216 | tf_op jit(solution)/shard_map/ppermute | solution.py:351
  6.7 15.6 %all-to-all-start = ((f32[16,16,128]{2,1,0:T(8,128)}), f32[16,16,128]{2,1,0:T(8,128)S(1)}, u32[]{:S(2)}, u32[]{:S(2)}) async-start(f32[16,16,128]{2,1,0:T(8,128)} %bitcast.18), calls=%async_computation | async-start | bytes 262144 | tf_op jit(solution)/shard_map/all_to_all | solution.py:380
  14.8 1.9 %copy-start.2 = (f32[16,128,384]{2,1,0:T(8,128)S(1)}, f32[16,128,384]{2,1,0:T(8,128)}, u32[]{:S(2)}) copy-start(f32[16,128,384]{2,1,0:T(8,128)} %leg_ref) | copy-start | bytes 9437188
  16.7 0.9 copy-start.14
  17.7 13.9 %collective-permute-start = (bf16[64,1536]{1,0:T(8,128)(2,1)S(1)}, bf16[64,1536]{1,0:T(8,128)(2,1)S(1)}, u32[]{:S(2)}, u32[]{:S(2)}) collective-permute-start(bf16[64,1536]{1,0:T(8,128)(2,1)S(1)} %reshape.42.own_ref), channel_id=1, source_target_pairs={{0,2},{2,0},{4,6},{6,4},{8,10},{10,8},{12,14},{14,12},{1,3},{3,1},... | collective-permute-start | bytes 589832 | tf_op jit(solution)/shard_map/ppermute | solution.py:354
  23.6 16.0 %all-to-all-start.1 = ((f32[16,8,640]{2,1,0:T(8,128)}), f32[16,8,640]{2,1,0:T(8,128)S(1)}, u32[]{:S(2)}, u32[]{:S(2)}) async-start(f32[16,8,640]{2,1,0:T(8,128)} %legendre.1), calls=%async_computation.1 | async-start | bytes 655360 | tf_op jit(solution)/shard_map/all_to_all | solution.py:410
  31.7 63.1 %copy-start = (bf16[128,1536]{1,0:T(8,128)(2,1)}, bf16[128,1536]{1,0:T(8,128)(2,1)S(1)}, u32[]{:S(2)}) copy-start(bf16[128,1536]{1,0:T(8,128)(2,1)S(1)} %pair.1.refs_8_) | copy-start | bytes 1179652
  31.7 31.0 %collective-permute-start.3 = (bf16[128,1536]{1,0:T(8,128)(2,1)S(1)}, bf16[128,1536]{1,0:T(8,128)(2,1)S(1)}, u32[]{:S(2)}, u32[]{:S(2)}) collective-permute-start(bf16[128,1536]{1,0:T(8,128)(2,1)S(1)} %pair.1.refs_8_), channel_id=1, source_target_pairs={{0,4},{2,6},{4,8},{6,10},{8,12},{10,14},{12,0},{14,2},{1,5},{3,7},... | collective-permute-start | bytes 1179656 | tf_op jit(solution)/shard_map/ppermute | solution.py:351
  32.1 31.4 %collective-permute-start.4 = (bf16[128,1536]{1,0:T(8,128)(2,1)S(1)}, bf16[128,1536]{1,0:T(8,128)(2,1)}, u32[]{:S(2)}, u32[]{:S(2)}) collective-permute-start(bf16[128,1536]{1,0:T(8,128)(2,1)S(1)} %pair.1.refs_8_), channel_id=1, source_target_pairs={{0,12},{2,14},{4,0},{6,2},{8,4},{10,6},{12,8},{14,10},{1,13},{3,15... | collective-permute-start | bytes 1179656 | tf_op jit(solution)/shard_map/ppermute | solution.py:351
  35.0 49.4 %collective-permute-start.5 = (bf16[288,1536]{1,0:T(8,128)(2,1)}, bf16[288,1536]{1,0:T(8,128)(2,1)}, u32[]{:S(2)}, u32[]{:S(2)}) collective-permute-start(bf16[288,1536]{1,0:T(8,128)(2,1)} %bitcast.5.refs_0_), channel_id=1, source_target_pairs={{0,8},{2,10},{4,12},{6,14},{8,0},{10,2},{12,4},{14,6},{1,9},{3,11}... | collective-permute-start | bytes 2654216 | tf_op jit(solution)/shard_map/ppermute | solution.py:351
  42.1 24.5 %all-to-all-start.2 = ((f32[16,8,128]{2,1,0:T(8,128)}), f32[16,8,128]{2,1,0:T(8,128)}, u32[]{:S(2)}, u32[]{:S(2)}) async-start(f32[16,8,128]{2,1,0:T(8,128)} %bitcast.7), calls=%async_computation.2 | async-start | bytes 131072 | tf_op jit(solution)/shard_map/all_to_all | solution.py:426
  49.0 43.3 %collective-permute-start.6 = (bf16[288,1536]{1,0:T(8,128)(2,1)}, bf16[288,1536]{1,0:T(8,128)(2,1)}, u32[]{:S(2)}, u32[]{:S(2)}) collective-permute-start(bf16[288,1536]{1,0:T(8,128)(2,1)} %bitcast.5.refs_0_), channel_id=1, source_target_pairs={{0,1},{1,0},{2,3},{3,2},{4,5},{5,4},{6,7},{7,6},{8,9},{9,8},{10,11... | collective-permute-start | bytes 2654216 | tf_op jit(solution)/shard_map/ppermute | solution.py:357
  62.7 0.8 copy-start.9
  63.5 1.4 %copy-start.3 = (bf16[512,1440]{1,0:T(8,128)(2,1)S(1)}, bf16[512,1440]{1,0:T(8,128)(2,1)}, u32[]{:S(2)}) copy-start(bf16[512,1440]{1,0:T(8,128)(2,1)} %constant.44.clone.table_ref) | copy-start | bytes 4423684
  64.9 1.4 %copy-start.4 = (bf16[512,1536]{1,0:T(8,128)(2,1)S(1)}, bf16[512,1536]{1,0:T(8,128)(2,1)}, u32[]{:S(2)}) copy-start(bf16[512,1536]{1,0:T(8,128)(2,1)} %constant.45.clone.cell_ref) | copy-start | bytes 4718596
  66.6 13.9 %copy-start.15 = (f32[1536]{0:T(1024)S(1)}, f32[1536]{0:T(1024)}, u32[]{:S(2)}) copy-start(f32[1536]{0:T(1024)} %param.16) | copy-start | bytes 18436
  68.7 0.7 copy-start.1
  69.4 19.0 %all-to-all-start.3 = ((bf16[16,48,128]{2,1,0:T(8,128)(2,1)}), bf16[16,48,128]{2,1,0:T(8,128)(2,1)S(1)}, u32[]{:S(2)}, u32[]{:S(2)}) async-start(bf16[16,48,128]{2,1,0:T(8,128)(2,1)} %copy-done.1), calls=%async_computation.3 | async-start | bytes 393216 | tf_op jit(solution)/shard_map/all_to_all | solution.py:457
  77.0 15.3 %collective-permute-start.10 = (bf16[128,1536]{1,0:T(8,128)(2,1)S(1)}, bf16[128,1536]{1,0:T(8,128)(2,1)}, u32[]{:S(2)}, u32[]{:S(2)}) collective-permute-start(bf16[128,1536]{1,0:T(8,128)(2,1)S(1)} %pair.1.refs_8_), channel_id=1, source_target_pairs={{0,8},{2,10},{4,12},{6,14},{8,0},{10,2},{12,4},{14,6},{1,9},{3,11}... | collective-permute-start | bytes 1179656 | tf_op jit(solution)/shard_map/ppermute | solution.py:351
  81.0 13.9 %collective-permute-start.7 = (bf16[288,1536]{1,0:T(8,128)(2,1)}, bf16[288,1536]{1,0:T(8,128)(2,1)S(1)}, u32[]{:S(2)}, u32[]{:S(2)}) collective-permute-start(bf16[288,1536]{1,0:T(8,128)(2,1)} %collective-permute-done.1.refs_1_), channel_id=1, source_target_pairs={{0,1},{1,0},{2,3},{3,2},{4,5},{5,4},{6,7},{7,6},{8,9},{9,8},{10,11... | collective-permute-start | bytes 2654216 | tf_op jit(solution)/shard_map/ppermute | solution.py:357
  81.0 13.9 %collective-permute-start.8 = (bf16[288,1536]{1,0:T(8,128)(2,1)}, bf16[288,1536]{1,0:T(8,128)(2,1)S(1)}, u32[]{:S(2)}, u32[]{:S(2)}) collective-permute-start(bf16[288,1536]{1,0:T(8,128)(2,1)} %collective-permute-done.2.refs_2_), channel_id=1, source_target_pairs={{0,1},{1,0},{2,3},{3,2},{4,5},{5,4},{6,7},{7,6},{8,9},{9,8},{10,11... | collective-permute-start | bytes 2654216 | tf_op jit(solution)/shard_map/ppermute | solution.py:357
  88.4 9.3 %copy-start.8 = (bf16[16,48,128]{2,1,0:T(8,128)(2,1)}, bf16[16,48,128]{2,1,0:T(8,128)(2,1)S(1)}, u32[]{:S(2)}) copy-start(bf16[16,48,128]{2,1,0:T(8,128)(2,1)S(1)} %all-to-all-done.3.cells_ref) | copy-start | bytes 589828
  88.4 9.3 %collective-permute-start.9 = (bf16[288,1536]{1,0:T(8,128)(2,1)}, bf16[288,1536]{1,0:T(8,128)(2,1)S(1)}, u32[]{:S(2)}, u32[]{:S(2)}) collective-permute-start(bf16[288,1536]{1,0:T(8,128)(2,1)} %collective-permute-done.5.refs_3_), channel_id=1, source_target_pairs={{0,1},{1,0},{2,3},{3,2},{4,5},{5,4},{6,7},{7,6},{8,9},{9,8},{10,11... | collective-permute-start | bytes 2654216 | tf_op jit(solution)/shard_map/ppermute | solution.py:357
  92.3 1.9 %collective-permute-start.12 = (bf16[128,1536]{1,0:T(8,128)(2,1)}, bf16[128,1536]{1,0:T(8,128)(2,1)S(1)}, u32[]{:S(2)}, u32[]{:S(2)}) collective-permute-start(bf16[128,1536]{1,0:T(8,128)(2,1)} %copy-done.9), channel_id=1, source_target_pairs={{0,1},{1,0},{2,3},{3,2},{4,5},{5,4},{6,7},{7,6},{8,9},{9,8},{10,11... | collective-permute-start | bytes 1179656 | tf_op jit(solution)/shard_map/ppermute | solution.py:357
  92.3 2.5 %collective-permute-start.13 = (bf16[128,1536]{1,0:T(8,128)(2,1)}, bf16[128,1536]{1,0:T(8,128)(2,1)S(1)}, u32[]{:S(2)}, u32[]{:S(2)}) collective-permute-start(bf16[128,1536]{1,0:T(8,128)(2,1)} %collective-permute-done.4.refs_10_), channel_id=1, source_target_pairs={{0,1},{1,0},{2,3},{3,2},{4,5},{5,4},{6,7},{7,6},{8,9},{9,8},{10,11... | collective-permute-start | bytes 1179656 | tf_op jit(solution)/shard_map/ppermute | solution.py:357
  94.2 3.5 %copy-start.10 = (bf16[128,1536]{1,0:T(8,128)(2,1)}, bf16[128,1536]{1,0:T(8,128)(2,1)S(1)}, u32[]{:S(2)}) copy-start(bf16[128,1536]{1,0:T(8,128)(2,1)S(1)} %collective-permute-done.12.refs_13_) | copy-start | bytes 1179652
  94.2 1.9 %collective-permute-start.14 = (bf16[128,1536]{1,0:T(8,128)(2,1)}, bf16[128,1536]{1,0:T(8,128)(2,1)S(1)}, u32[]{:S(2)}, u32[]{:S(2)}) collective-permute-start(bf16[128,1536]{1,0:T(8,128)(2,1)} %collective-permute-done.10.refs_11_), channel_id=1, source_target_pairs={{0,1},{1,0},{2,3},{3,2},{4,5},{5,4},{6,7},{7,6},{8,9},{9,8},{10,11... | collective-permute-start | bytes 1179656 | tf_op jit(solution)/shard_map/ppermute | solution.py:357
  94.8 1.7 %copy-start.11 = (bf16[128,1536]{1,0:T(8,128)(2,1)}, bf16[128,1536]{1,0:T(8,128)(2,1)S(1)}, u32[]{:S(2)}) copy-start(bf16[128,1536]{1,0:T(8,128)(2,1)S(1)} %collective-permute-done.13.refs_14_) | copy-start | bytes 1179652
  94.8 1.7 %collective-permute-start.11 = (bf16[128,1536]{1,0:T(8,128)(2,1)S(1)}, bf16[128,1536]{1,0:T(8,128)(2,1)S(1)}, u32[]{:S(2)}, u32[]{:S(2)}) collective-permute-start(bf16[128,1536]{1,0:T(8,128)(2,1)S(1)} %pair.1.refs_8_), channel_id=1, source_target_pairs={{0,1},{1,0},{2,3},{3,2},{4,5},{5,4},{6,7},{7,6},{8,9},{9,8},{10,11... | collective-permute-start | bytes 1179656 | tf_op jit(solution)/shard_map/ppermute | solution.py:357
  94.9 2.8 %copy-start.5 = (bf16[288,1536]{1,0:T(8,128)(2,1)}, bf16[288,1536]{1,0:T(8,128)(2,1)S(1)}, u32[]{:S(2)}) copy-start(bf16[288,1536]{1,0:T(8,128)(2,1)S(1)} %collective-permute-done.7.refs_5_) | copy-start | bytes 2654212
  94.9 2.8 %copy-start.6 = (bf16[288,1536]{1,0:T(8,128)(2,1)}, bf16[288,1536]{1,0:T(8,128)(2,1)S(1)}, u32[]{:S(2)}) copy-start(bf16[288,1536]{1,0:T(8,128)(2,1)S(1)} %collective-permute-done.8.refs_6_) | copy-start | bytes 2654212
  96.1 0.7 copy-start.12
  96.9 0.8 copy-start.13
  97.7 0.9 copy-start.7
  112.4 19.7 %all-to-all-start.4 = ((bf16[16,72,128]{2,1,0:T(8,128)(2,1)}), bf16[16,72,128]{2,1,0:T(8,128)(2,1)S(1)}, u32[]{:S(2)}, u32[]{:S(2)}) async-start(bf16[16,72,128]{2,1,0:T(8,128)(2,1)} %bitcast.17), calls=%async_computation.4 | async-start | bytes 589824 | tf_op jit(solution)/shard_map/all_to_all | solution.py:479
